TPU v7x, 32 devices: a whole 2x2x4 slice. The times are simulated.
32 devices in a mesh: row: 4 (over y, x), col: 8 (over z, core).
Axes of the slice: x: 2, y: 2, z: 4, core: 2. Of those that a mesh axis runs over, the one named last changes fastest.
Arguments:
- panel: float32 [3072, 8192], P('row', 'col'), may hold values from -6 to 6
- row_weights: float32 [3072], P('row'), may hold values from 0.25 to 4
Outputs:
- normal_matrix: float32 [8192, 8192], P('row', 'col')
All inputs are finite; a program needn't handle non-finite values.
Results may differ from a plain program's by a relative error of at most 0.00011.
Values sent between devices are 32-bit elements; how exact they have to be, the bound alone decides.
No kernel may reach another device: no remote copies, remote signals or barrier semaphores. Data moves between devices by JAX's collectives and lax.ppermute only.
A program may use at most 192 MiB of HBM per device.

v0:
```python
import jax
import jax.numpy as jnp
from jax import lax
from jax.sharding import PartitionSpec as P


def local(panel, row_weights):
    total_rows = panel.shape[0] * lax.axis_size("row")
    weighted = row_weights[:, None] * panel
    partial_sum = jnp.dot(
        lax.all_gather(weighted, "col", axis=1, tiled=True).T,
        panel,
        preferred_element_type=jnp.float32,
        precision=lax.Precision.HIGHEST,
    )
    summed = lax.psum_scatter(partial_sum, "row", scatter_dimension=0, tiled=True)
    return summed * (1.0 / total_rows)


def solution(mesh):
    return jax.shard_map(
        local,
        mesh=mesh,
        in_specs=(P("row", "col"), P("row")),
        out_specs=P("row", "col"),
        check_vma=False,
    )
```

profile of v0, /device:TPU:0, one launch (start us, length us, event | category | flops | bytes accessed | tf_op | source)
XLA Modules:
  0.0 622.0 jit_solution(11453656628550765782)
XLA Ops:
  6.5 0.0 copy-start
  6.5 0.0 all-gather.2.cloned.1.call-start
  6.5 4.0 broadcast_multiply_fusion.1
  10.5 0.0 all-gather.2.cloned.1.call-update
  10.5 0.0 reduce-scatter.2.cloned.1.call-start
  10.6 222.7 %all-gather.2.cloned.1.call-done = f32[768,8192]{1,0:T(8,128)} async-done(((f32[768,1024]{1,0:T(8,128)}), f32[768,8192]{1,0:T(8,128)}) %all-gather.2.cloned.1.call-update) | async-done | bytes 25165840 | tf_op jit(solution)/shard_map/all_gather | solution.py:11
  233.3 0.0 copy-done
  233.3 86.1 %fusion = f32[8192,1024]{1,0:T(8,128)} fusion(f32[768,8192]{1,0:T(8,128)} %all-gather.2.cloned.1.call-done, f32[768,1024]{1,0:T(8,128)S(1)} %copy-done), kind=kOutput, calls=%fused_computation.2 | convolution fusion | flops 77309411328 | bytes 61865984 | tf_op jit(solution)/shard_map/dot_general | solution.py:10
  319.4 0.0 reduce-scatter.2.cloned.1.call-update
  319.4 287.0 %reduce-scatter.2.cloned.1.call-done = f32[2048,1024]{1,0:T(8,128)} async-done(((f32[8192,1024]{1,0:T(8,128)}), f32[2048,1024]{1,0:T(8,128)}) %reduce-scatter.2.cloned.1.call-update) | async-done | bytes 8388624 | tf_op jit(solution)/shard_map/reduce_scatter | solution.py:16
  606.4 8.8 %broadcast_multiply_fusion = f32[2048,1024]{1,0:T(8,128)} fusion(f32[2048,1024]{1,0:T(8,128)} %reduce-scatter.2.cloned.1.call-done), kind=kLoop, calls=%fused_computation | loop fusion | flops 2097152 | bytes 16777216 | tf_op jit(solution)/shard_map/mul | solution.py:17
Async XLA Ops:
  6.5 226.7 %copy-start = (f32[768,1024]{1,0:T(8,128)S(1)}, f32[768,1024]{1,0:T(8,128)}, u32[]{:S(2)}) copy-start(f32[768,1024]{1,0:T(8,128)} %param.2) | copy-start | bytes 9437188
  6.5 226.7 %all-gather.2.cloned.1.call-start = ((), (), s32[]{:S(2)}) async-start(), calls=%async_computation.1 | async-start | bytes 28311552 | tf_op jit(solution)/shard_map/all_gather | solution.py:11
  10.5 595.9 %reduce-scatter.2.cloned.1.call-start = ((), (), s32[]{:S(2)}) async-start(), calls=%async_computation.2 | async-start | bytes 41943040 | tf_op jit(solution)/shard_map/reduce_scatter | solution.py:16
Sparse Core Ops, SparseCore 0:
  10.7 222.5 all-gather.1
  319.5 286.8 reduce-scatter.1
where the time goes:
time: 622 us
  waiting for transfers between devices  510 us (82%)
  matrix products  86.1 us (14%)
  between operations  13.4 us (2%)
  other arithmetic  12.8 us (2%)
    reduce_scatter x1, waiting for transfers between devices, local(): lax.psum_scatter(partial_sum, 'row', scatter_dimension=0, tiled=True)  287 us
    all_gather x1, waiting for transfers between devices, local(): lax.all_gather(weighted, 'col', axis=1, tiled=True)  223 us
    dot_general x1, matrix products, local(): jnp.dot(lax.all_gather(weighted, 'col', axis=1, tiled=True).T, panel, pre...  86.1 us
  transfers between devices with their start and end apart: 2, of which 2 were waited for; matrix products, arithmetic and copies ran while one was open for 0% of the time, Pallas kernels for 0%

commit v1 on v0

--- a/solution.py
+++ b/solution.py
@@ -1,10 +1,15 @@
 import jax
 import jax.numpy as jnp
 from jax import lax
+from jax.experimental import pallas as pl
+from jax.experimental.pallas import tpu as pltpu
 from jax.sharding import PartitionSpec as P
 
+PARTS = (2, 2, 2, 1, 1)
+AXES = ("row", "col")
 
-def local(panel, row_weights):
+
+def plain(panel, row_weights):
     total_rows = panel.shape[0] * lax.axis_size("row")
     weighted = row_weights[:, None] * panel
     partial_sum = jnp.dot(
@@ -17,9 +22,134 @@
     return summed * (1.0 / total_rows)
 
 
+def product_body(count, where_ref, mine_ref, other_ref, *refs):
+    right_refs, out_ref, hi_ref, lo_ref = refs[:count], refs[-3], refs[-2], refs[-1]
+    r, k = where_ref[0], where_ref[1]
+    m = mine_ref.shape[1]
+
+    @pl.when(pl.program_id(0) == 0)
+    def _():
+        for side, ref in enumerate((mine_ref, other_ref)):
+            for e in range(count):
+                x = ref[lax.bitwise_xor(r, e)]
+                hi = x.astype(jnp.bfloat16)
+                hi_ref[e, side * m : (side + 1) * m] = hi
+                lo_ref[e, side * m : (side + 1) * m] = (x - hi.astype(jnp.float32)).astype(jnp.bfloat16)
+
+    def dot(a, b):
+        return jnp.dot(a, b, preferred_element_type=jnp.float32)
+
+    total = None
+    for e in range(count):
+        right = right_refs[e][...]
+        hi = right.astype(jnp.bfloat16)
+        lo = (right - hi.astype(jnp.float32)).astype(jnp.bfloat16)
+        term = dot(hi_ref[e], hi) + (dot(hi_ref[e], lo) + dot(lo_ref[e], hi))
+        total = term if total is None else total + term
+    out_ref[k] = total[:m]
+    out_ref[1 - k] = total[m:]
+
+
+def product(where, mine, other, rights, out, start, tile=256):
+    count, m, depth = mine.shape
+    height = rights[0].shape[1]
+    width = rights[0].shape[1]
+    assert start % m == 0
+    whole_left = pl.BlockSpec((count, m, depth), lambda j, s: (0, 0, 0))
+    in_specs = [whole_left, whole_left]
+    in_specs += [pl.BlockSpec((depth, tile), lambda j, s: (0, j)) for _ in rights]
+    args = [where, mine, other, *rights]
+    aliases = {}
+    if out is not None:
+        in_specs.append(pl.BlockSpec(memory_space=pl.ANY))
+        args.append(out)
+        aliases = {len(args) - 1: 0}
+
+    def body(where_ref, mine_ref, other_ref, *refs):
+        product_body(count, where_ref, mine_ref, other_ref, *refs)
+
+    return pl.pallas_call(
+        body,
+        out_shape=jax.ShapeDtypeStruct((2, height, width), jnp.float32),
+        grid_spec=pltpu.PrefetchScalarGridSpec(
+            num_scalar_prefetch=1,
+            grid=(width // tile,),
+            in_specs=in_specs,
+            out_specs=pl.BlockSpec((2, m, tile), lambda j, s: (0, start // m, j)),
+            scratch_shapes=[pltpu.VMEM((count, 2 * m, depth), jnp.bfloat16)] * 2,
+        ),
+        input_output_aliases=aliases,
+        compiler_params=pltpu.CompilerParams(vmem_limit_bytes=50 << 20),
+        cost_estimate=pl.CostEstimate(
+            flops=6 * 2 * m * width * depth * count,
+            bytes_accessed=4 * (2 * count * m * depth + count * depth * width + 2 * m * width),
+            transcendentals=0,
+        ),
+    )(*args)
+
+
+def exchange(panel, row_weights):
+    n = lax.axis_size("row")
+    cols = lax.axis_size("col")
+    r = lax.axis_index("row")
+    k = lax.axis_index("col") % 2
+    where = jnp.stack([r, k]).astype(jnp.int32)
+    rows, width = panel.shape
+
+    def across(x, e):
+        moves = [(a * cols + b, (a ^ e) * cols + b) for a in range(n) for b in range(cols)]
+        return lax.ppermute(x, AXES, moves)
+
+    def swap(x):
+        moves = [(a * cols + b, a * cols + (b ^ 1)) for a in range(n) for b in range(cols)]
+        return lax.ppermute(x, AXES, moves)
+
+    scale = jnp.sqrt(row_weights * (1.0 / (rows * n)))
+    own = panel * scale[:, None]
+
+    rights = [own]
+    half = width // 2
+    for e in range(1, n):
+        top = 1 << (e.bit_length() - 1)
+        low = e & -e
+        if top == low:
+            rights.append(across(own, e))
+        else:
+            parts = [across(rights[e ^ top][:, :half], top), across(rights[e ^ low][:, half:], low)]
+            rights.append(jnp.concatenate(parts, axis=1))
+
+    groups = [[b for b in range(cols) if b % 2 == core] for core in (0, 1)]
+    unit = width // sum(PARTS)
+    starts = [unit * sum(PARTS[:i]) for i in range(len(PARTS))]
+    outs, arrived = [None], []
+
+    def finish(i):
+        outs.append(product(where, arrived[i], swap(arrived[i]), rights, outs[-1], starts[i]))
+
+    for i, part in enumerate(PARTS):
+        piece = lax.slice_in_dim(panel, starts[i], starts[i] + part * unit, axis=1).T * scale
+        if i >= 2:
+            piece, arrived[i - 2] = lax.optimization_barrier((piece, arrived[i - 2]))
+        if i == 2:
+            piece, rights[:3] = lax.optimization_barrier((piece, rights[:3]))
+        if i == 3:
+            piece, rights = lax.optimization_barrier((piece, rights))
+        line = lax.all_gather(piece, "col", axis=0, axis_index_groups=groups)
+        if i >= 2:
+            finish(i - 2)
+            line, outs[-1] = lax.optimization_barrier((line, outs[-1]))
+        arrived.append(lax.all_to_all(line, "row", 0, 0))
+    for i in range(len(PARTS) - 2, len(PARTS)):
+        finish(i)
+    out = outs[-1]
+    return out.reshape(2 * width, width)
+
+
 def solution(mesh):
+    n, cols = mesh.shape["row"], mesh.shape["col"]
+    paired = cols == 2 * n and n & (n - 1) == 0 and n > 1
     return jax.shard_map(
-        local,
+        exchange if paired else plain,
         mesh=mesh,
         in_specs=(P("row", "col"), P("row")),
         out_specs=P("row", "col"),

time: 622 us -> 361 us (0.58)
  waiting for transfers between devices: 510 us -> 176 us
  matrix products: 86.1 us -> 0 us
  Pallas kernels: 0 us -> 70.5 us
  blocking collectives: 0 us -> 42.2 us
  local copies, waits for them, and re-layouts: 0.01 us -> 26.9 us
  starting transfers between devices: 0.04 us -> 22.2 us
    reduce_scatter x1 -> x0, waiting for transfers between devices: 287 us -> none  [local(): lax.psum_scatter(partial_sum, 'row', scatter_dimension=0, tiled=True)]
    all_gather x1 -> x5, waiting for transfers between devices: 223 us -> 105 us  [exchange(): line = lax.all_gather(piece, 'col', axis=0, axis_index_groups=groups)]
    dot_general x1 -> x0, matrix products: 86.1 us -> none  [local(): jnp.dot(lax.all_gather(weighted, 'col', axis=1, tiled=True).T, panel, pre...]
    pallas_call x0 -> x5, Pallas kernels: none -> 70.5 us  [product(): pl.pallas_call(body, out_shape=jax.ShapeDtypeStruct((2, height, width), j...]
    all_to_all x0 -> x4, waiting for transfers between devices: none -> 53.5 us  [exchange(): arrived.append(lax.all_to_all(line, 'row', 0, 0))]
    all_to_all x0 -> x1, blocking collectives: none -> 42.2 us  [exchange(): arrived.append(lax.all_to_all(line, 'row', 0, 0))]
    ppermute x0 -> x9, waiting for transfers between devices: none -> 16.9 us  [the longest x4 16.9 us: across(): return lax.ppermute(x, AXES, moves)]
    all_gather x0 -> x5, local copies, waits for them, and re-layouts: none -> 16.8 us  [exchange(): line = lax.all_gather(piece, 'col', axis=0, axis_index_groups=groups)]
  transfers between devices with their start and end apart: 2 -> 18, of which waited for: 2 -> 9; matrix products, arithmetic and copies ran while one was open for 0% -> 8% of each run, Pallas kernels for 0% -> 17%
where the time goes in v1:
time: 361 us; the launch traced here: 360 us
  waiting for transfers between devices  176 us (49%)
  Pallas kernels  70.5 us (20%)
  blocking collectives  42.2 us (12%)
  local copies, waits for them, and re-layouts  26.9 us (7%)
  starting transfers between devices  22.2 us (6%)
  between operations  13.3 us (4%)
  other arithmetic  8.41 us (2%)
    all_gather x5, waiting for transfers between devices, exchange(): line = lax.all_gather(piece, 'col', axis=0, axis_index_groups=groups)  105 us
    pallas_call x5, Pallas kernels, product(): pl.pallas_call(body, out_shape=jax.ShapeDtypeStruct((2, height, width), j...  70.5 us
    all_to_all x4, waiting for transfers between devices, exchange(): arrived.append(lax.all_to_all(line, 'row', 0, 0))  53.5 us
    all_to_all x1, blocking collectives, exchange(): arrived.append(lax.all_to_all(line, 'row', 0, 0))  42.2 us
    ppermute x4, waiting for transfers between devices, across(): return lax.ppermute(x, AXES, moves)  16.9 us
    all_gather x5, local copies, waits for them, and re-layouts, exchange(): line = lax.all_gather(piece, 'col', axis=0, axis_index_groups=groups)  16.8 us
    all_to_all x4, starting transfers between devices, exchange(): arrived.append(lax.all_to_all(line, 'row', 0, 0))  15.8 us
  transfers between devices with their start and end apart: 18, of which 9 were waited for; matrix products, arithmetic and copies ran while one was open for 8% of the time, Pallas kernels for 17%

profile of v1, /device:TPU:0, one launch (start us, length us, event | category | flops | bytes accessed | tf_op | source)
XLA Modules:
  0.0 359.6 jit_solution(14177608113354031537)
XLA Ops:
  7.2 3.3 multiply_bitcast_fusion
  13.5 3.0 collective-permute-start
  18.0 58.8 %all-gather.11.cloned.1.call-done = f32[1024,768]{0,1:T(8,128)} async-done(((f32[256,768]{0,1:T(8,128)}), f32[1024,768]{0,1:T(8,128)}) %all-gather.11.cloned.1.call-update) | async-done | bytes 3145744 | tf_op jit(solution)/shard_map/all_gather | solution.py:137
  76.8 3.5 copy.7
  80.4 42.2 %all_to_all.25.mine_ref = f32[4,256,768]{2,1,0:T(8,128)} all-to-all(f32[4,256,768]{2,1,0:T(8,128)} %bitcast.20), channel_id=1, replica_groups=mesh['row'=4,'col'=8] {'row'}, dimensions={0} | all-to-all | bytes 6291456 | tf_op jit(solution)/shard_map/all_to_all | solution.py:141
  129.5 11.1 %all-gather.17.cloned.1.call-done = f32[1024,768]{0,1:T(8,128)} async-done(((f32[256,768]{0,1:T(8,128)}), f32[1024,768]{0,1:T(8,128)}) %all-gather.17.cloned.1.call-update) | async-done | bytes 3145744 | tf_op jit(solution)/shard_map/all_gather | solution.py:137
  140.6 3.6 %copy.10 = f32[1024,768]{1,0:T(8,128)} copy(f32[1024,768]{0,1:T(8,128)} %all-gather.17.cloned.1.call-done) | data formatting | bytes 6291456 | tf_op jit(solution)/shard_map/all_gather | solution.py:137
  144.2 3.7 %all-to-all-start.2 = ((f32[4,256,768]{2,1,0:T(8,128)}), f32[4,256,768]{2,1,0:T(8,128)S(1)}, u32[]{:S(2)}, u32[]{:S(2)}) async-start(f32[4,256,768]{2,1,0:T(8,128)} %bitcast.18), calls=%async_computation.2 | async-start | bytes 6291456 | tf_op jit(solution)/shard_map/all_to_all | solution.py:141
  148.0 14.9 %collective-permute-done.3 = f32[768,512]{1,0:T(8,128)} collective-permute-done((f32[768,512]{1,0:T(8,128)}, f32[768,512]{1,0:T(8,128)}, u32[]{:S(2)}, u32[]{:S(2)}) %collective-permute-start.3) | collective-permute-done | bytes 1572896 | tf_op jit(solution)/shard_map/ppermute | solution.py:101
  169.8 16.9 %shard_map.28.refs_4_ = f32[2,1024,1024]{2,1,0:T(8,128)} custom-call(s32[2]{0:T(128)S(1)} %pad_add_fusion.where_ref, f32[4,256,768]{2,1,0:T(8,128)} %all_to_all.25.mine_ref, f32[4,256,768]{2,1,0:T(8,128)} %collective-permute-done.2.other_ref, f32[768,1024]{1,0:T(8,128)} %copy-done, f32[768,1024]{1,0:T(8,128)} %collective-permute-done.refs_1_, ...), custom_call_target="tpu_custom_call" | custom-call | flops 9663676416 | bytes 20971520 | tf_op jit(solution)/shard_map/pallas_call | solution.py:71
  186.6 17.7 %all-gather.13.cloned.1.call-done = f32[1024,768]{0,1:T(8,128)} async-done(((f32[256,768]{0,1:T(8,128)}), f32[1024,768]{0,1:T(8,128)}) %all-gather.13.cloned.1.call-update) | async-done | bytes 3145744 | tf_op jit(solution)/shard_map/all_gather | solution.py:137
  204.3 3.5 copy.8
  207.9 4.7 %all-to-all-start.1 = ((f32[4,256,768]{2,1,0:T(8,128)}), f32[4,256,768]{2,1,0:T(8,128)}, u32[]{:S(2)}, u32[]{:S(2)}) async-start(f32[4,256,768]{2,1,0:T(8,128)} %bitcast.19), calls=%async_computation.1 | async-start | bytes 6291456 | tf_op jit(solution)/shard_map/all_to_all | solution.py:141
  215.0 34.0 %all-to-all-done.1.mine_ref = f32[4,256,768]{2,1,0:T(8,128)} async-done(((f32[4,256,768]{2,1,0:T(8,128)}), f32[4,256,768]{2,1,0:T(8,128)}, u32[]{:S(2)}, u32[]{:S(2)}) %all-to-all-start.1) | async-done | bytes 3145760 | tf_op jit(solution)/shard_map/all_to_all | solution.py:141
  251.9 3.1 copy.11
  254.9 16.0 %shard_map.29.refs_4_ = f32[2,1024,1024]{2,1,0:T(8,128)} custom-call(s32[2]{0:T(128)S(1)} %pad_add_fusion.where_ref, f32[4,256,768]{2,1,0:T(8,128)S(1)} %all-to-all-done.2.mine_ref, f32[4,256,768]{2,1,0:T(8,128)} %collective-permute-done.6.other_ref, f32[768,1024]{1,0:T(8,128)} %copy-done, ...), custom_call_target="tpu_custom_call", output_to_operand_aliasing={{}: (7, {})} | custom-call | flops 9663676416 | bytes 20971520 | tf_op jit(solution)/shard_map/pallas_call | solution.py:71
  270.9 3.7 %all-to-all-start.4 = ((f32[4,128,768]{2,1,0:T(8,128)}), f32[4,128,768]{2,1,0:T(8,128)S(1)}, u32[]{:S(2)}, u32[]{:S(2)}) async-start(f32[4,128,768]{2,1,0:T(8,128)} %bitcast.21), calls=%async_computation.4 | async-start | bytes 3145728 | tf_op jit(solution)/shard_map/all_to_all | solution.py:141
  274.7 14.6 %all-gather.15.cloned.1.call-done = f32[512,768]{0,1:T(8,128)} async-done(((f32[128,768]{0,1:T(8,128)}), f32[512,768]{0,1:T(8,128)}) %all-gather.15.cloned.1.call-update) | async-done | bytes 1572880 | tf_op jit(solution)/shard_map/all_gather | solution.py:137
  289.3 3.0 copy.9
  292.3 16.8 %shard_map.30.refs_4_ = f32[2,1024,1024]{2,1,0:T(8,128)} custom-call(s32[2]{0:T(128)S(1)} %pad_add_fusion.where_ref, f32[4,256,768]{2,1,0:T(8,128)} %all-to-all-done.1.mine_ref, f32[4,256,768]{2,1,0:T(8,128)} %collective-permute-done.5.other_ref, f32[768,1024]{1,0:T(8,128)} %copy-done, ...), custom_call_target="tpu_custom_call", output_to_operand_aliasing={{}: (7, {})} | custom-call | flops 9663676416 | bytes 20971520 | tf_op jit(solution)/shard_map/pallas_call | solution.py:71
  309.1 3.7 %all-to-all-start.3 = ((f32[4,128,768]{2,1,0:T(8,128)}), f32[4,128,768]{2,1,0:T(8,128)S(1)}, u32[]{:S(2)}, u32[]{:S(2)}) async-start(f32[4,128,768]{2,1,0:T(8,128)} %bitcast.22), calls=%async_computation.3 | async-start | bytes 3145728 | tf_op jit(solution)/shard_map/all_to_all | solution.py:141
  312.8 19.5 %all-to-all-done.3.mine_ref = f32[4,128,768]{2,1,0:T(8,128)S(1)} async-done(((f32[4,128,768]{2,1,0:T(8,128)}), f32[4,128,768]{2,1,0:T(8,128)S(1)}, u32[]{:S(2)}, u32[]{:S(2)}) %all-to-all-start.3) | async-done | bytes 1572896 | tf_op jit(solution)/shard_map/all_to_all | solution.py:141
  332.3 10.8 %shard_map.31.refs_4_ = f32[2,1024,1024]{2,1,0:T(8,128)} custom-call(s32[2]{0:T(128)S(1)} %pad_add_fusion.where_ref, f32[4,128,768]{2,1,0:T(8,128)S(1)} %all-to-all-done.4.mine_ref, f32[4,128,768]{2,1,0:T(8,128)} %collective-permute-done.8.other_ref, f32[768,1024]{1,0:T(8,128)} %copy-done, ...), custom_call_target="tpu_custom_call", output_to_operand_aliasing={{}: (7, {})} | custom-call | flops 4831838208 | bytes 16777216 | tf_op jit(solution)/shard_map/pallas_call | solution.py:71
  343.1 10.0 %shard_map.32 = f32[2,1024,1024]{2,1,0:T(8,128)} custom-call(s32[2]{0:T(128)S(1)} %pad_add_fusion.where_ref, f32[4,128,768]{2,1,0:T(8,128)S(1)} %all-to-all-done.3.mine_ref, f32[4,128,768]{2,1,0:T(8,128)S(1)} %collective-permute-done.7.other_ref, f32[768,1024]{1,0:T(8,128)} %copy-done, ...), custom_call_target="tpu_custom_call", output_to_operand_aliasing={{}: (7, {})} | custom-call | flops 4831838208 | bytes 16777216 | tf_op jit(solution)/shard_map/pallas_call | solution.py:71
  (41 shorter events, 24.3 us)
Async XLA Ops:
  6.5 70.3 %all-gather.11.cloned.1.call-start = ((), (), s32[]{:S(2)}) async-start(), calls=%async_computation.5 | async-start | bytes 3932160 | tf_op jit(solution)/shard_map/all_gather | solution.py:137
  10.5 130.1 %all-gather.17.cloned.1.call-start = ((), (), s32[]{:S(2)}) async-start(), calls=%async_computation.8 | async-start | bytes 3932160 | tf_op jit(solution)/shard_map/all_gather | solution.py:137
  11.3 193.1 %all-gather.13.cloned.1.call-start = ((), (), s32[]{:S(2)}) async-start(), calls=%async_computation.6 | async-start | bytes 3932160 | tf_op jit(solution)/shard_map/all_gather | solution.py:137
  13.5 66.9 %copy-start = (f32[768,1024]{1,0:T(8,128)}, f32[768,1024]{1,0:T(8,128)S(1)}, u32[]{:S(2)}) copy-start(f32[768,1024]{1,0:T(8,128)S(1)} %broadcast_multiply_fusion.refs_0_) | copy-start | bytes 9437188
  13.5 109.1 %collective-permute-start = (f32[768,1024]{1,0:T(8,128)S(1)}, f32[768,1024]{1,0:T(8,128)}, u32[]{:S(2)}, u32[]{:S(2)}) collective-permute-start(f32[768,1024]{1,0:T(8,128)S(1)} %broadcast_multiply_fusion.refs_0_), channel_id=1, source_target_pairs={{0,8},{1,9},{2,10},{3,11},{4,12},{5,13},{6,14},{7,15},{8,0},{9,1},... | collective-permute-start | bytes 9437192 | tf_op jit(solution)/shard_map/ppermute | solution.py:101
  16.5 106.1 %collective-permute-start.1 = (f32[768,1024]{1,0:T(8,128)S(1)}, f32[768,1024]{1,0:T(8,128)}, u32[]{:S(2)}, u32[]{:S(2)}) collective-permute-start(f32[768,1024]{1,0:T(8,128)S(1)} %broadcast_multiply_fusion.refs_0_), channel_id=1, source_target_pairs={{0,16},{1,17},{2,18},{3,19},{4,20},{5,21},{6,22},{7,23},{8,24},{9,... | collective-permute-start | bytes 9437192 | tf_op jit(solution)/shard_map/ppermute | solution.py:101
  122.6 45.5 %collective-permute-start.2 = (f32[4,256,768]{2,1,0:T(8,128)}, f32[4,256,768]{2,1,0:T(8,128)}, u32[]{:S(2)}, u32[]{:S(2)}) collective-permute-start(f32[4,256,768]{2,1,0:T(8,128)} %all_to_all.25.mine_ref), channel_id=1, source_target_pairs={{0,1},{1,0},{2,3},{3,2},{4,5},{5,4},{6,7},{7,6},{8,9},{9,8},{10,11... | collective-permute-start | bytes 9437192 | tf_op jit(solution)/shard_map/ppermute | solution.py:105
  125.4 37.5 %collective-permute-start.3 = (f32[768,512]{1,0:T(8,128)}, f32[768,512]{1,0:T(8,128)}, u32[]{:S(2)}, u32[]{:S(2)}) collective-permute-start(f32[768,512]{1,0:T(8,128)} %slice.28), channel_id=1, source_target_pairs={{0,16},{1,17},{2,18},{3,19},{4,20},{5,21},{6,22},{7,23},{8,24},{9,... | collective-permute-start | bytes 4718600 | tf_op jit(solution)/shard_map/ppermute | solution.py:101
  128.9 37.5 %collective-permute-start.4 = (f32[768,512]{1,0:T(8,128)}, f32[768,512]{1,0:T(8,128)}, u32[]{:S(2)}, u32[]{:S(2)}) collective-permute-start(f32[768,512]{1,0:T(8,128)} %slice.29), channel_id=1, source_target_pairs={{0,8},{1,9},{2,10},{3,11},{4,12},{5,13},{6,14},{7,15},{8,0},{9,1},... | collective-permute-start | bytes 4718600 | tf_op jit(solution)/shard_map/ppermute | solution.py:101
  144.2 63.7 %all-to-all-start.2 = ((f32[4,256,768]{2,1,0:T(8,128)}), f32[4,256,768]{2,1,0:T(8,128)S(1)}, u32[]{:S(2)}, u32[]{:S(2)}) async-start(f32[4,256,768]{2,1,0:T(8,128)} %bitcast.18), calls=%async_computation.2 | async-start | bytes 6291456 | tf_op jit(solution)/shard_map/all_to_all | solution.py:141
  168.1 1.7 copy-start.1
  207.9 41.1 %all-to-all-start.1 = ((f32[4,256,768]{2,1,0:T(8,128)}), f32[4,256,768]{2,1,0:T(8,128)}, u32[]{:S(2)}, u32[]{:S(2)}) async-start(f32[4,256,768]{2,1,0:T(8,128)} %bitcast.19), calls=%async_computation.1 | async-start | bytes 6291456 | tf_op jit(solution)/shard_map/all_to_all | solution.py:141
  212.6 39.3 %all-gather.19.cloned.1.call-start = ((), (), s32[]{:S(2)}) async-start(), calls=%async_computation.9 | async-start | bytes 1966080 | tf_op jit(solution)/shard_map/all_gather | solution.py:137
  214.9 74.4 %all-gather.15.cloned.1.call-start = ((), (), s32[]{:S(2)}) async-start(), calls=%async_computation.7 | async-start | bytes 1966080 | tf_op jit(solution)/shard_map/all_gather | solution.py:137
  214.9 40.0 %collective-permute-start.6 = (f32[4,256,768]{2,1,0:T(8,128)S(1)}, f32[4,256,768]{2,1,0:T(8,128)}, u32[]{:S(2)}, u32[]{:S(2)}) collective-permute-start(f32[4,256,768]{2,1,0:T(8,128)S(1)} %all-to-all-done.2.mine_ref), channel_id=1, source_target_pairs={{0,1},{1,0},{2,3},{3,2},{4,5},{5,4},{6,7},{7,6},{8,9},{9,8},{10,11... | collective-permute-start | bytes 9437192 | tf_op jit(solution)/shard_map/ppermute | solution.py:105
  249.0 43.3 %collective-permute-start.5 = (f32[4,256,768]{2,1,0:T(8,128)}, f32[4,256,768]{2,1,0:T(8,128)}, u32[]{:S(2)}, u32[]{:S(2)}) collective-permute-start(f32[4,256,768]{2,1,0:T(8,128)} %all-to-all-done.1.mine_ref), channel_id=1, source_target_pairs={{0,1},{1,0},{2,3},{3,2},{4,5},{5,4},{6,7},{7,6},{8,9},{9,8},{10,11... | collective-permute-start | bytes 9437192 | tf_op jit(solution)/shard_map/ppermute | solution.py:105
  270.9 38.2 %all-to-all-start.4 = ((f32[4,128,768]{2,1,0:T(8,128)}), f32[4,128,768]{2,1,0:T(8,128)S(1)}, u32[]{:S(2)}, u32[]{:S(2)}) async-start(f32[4,128,768]{2,1,0:T(8,128)} %bitcast.21), calls=%async_computation.4 | async-start | bytes 3145728 | tf_op jit(solution)/shard_map/all_to_all | solution.py:141
  309.1 23.2 %all-to-all-start.3 = ((f32[4,128,768]{2,1,0:T(8,128)}), f32[4,128,768]{2,1,0:T(8,128)S(1)}, u32[]{:S(2)}, u32[]{:S(2)}) async-start(f32[4,128,768]{2,1,0:T(8,128)} %bitcast.22), calls=%async_computation.3 | async-start | bytes 3145728 | tf_op jit(solution)/shard_map/all_to_all | solution.py:141
  312.8 19.5 %collective-permute-start.8 = (f32[4,128,768]{2,1,0:T(8,128)S(1)}, f32[4,128,768]{2,1,0:T(8,128)}, u32[]{:S(2)}, u32[]{:S(2)}) collective-permute-start(f32[4,128,768]{2,1,0:T(8,128)S(1)} %all-to-all-done.4.mine_ref), channel_id=1, source_target_pairs={{0,1},{1,0},{2,3},{3,2},{4,5},{5,4},{6,7},{7,6},{8,9},{9,8},{10,11... | collective-permute-start | bytes 4718600 | tf_op jit(solution)/shard_map/ppermute | solution.py:105
  332.3 10.8 %collective-permute-start.7 = (f32[4,128,768]{2,1,0:T(8,128)S(1)}, f32[4,128,768]{2,1,0:T(8,128)S(1)}, u32[]{:S(2)}, u32[]{:S(2)}) collective-permute-start(f32[4,128,768]{2,1,0:T(8,128)S(1)} %all-to-all-done.3.mine_ref), channel_id=1, source_target_pairs={{0,1},{1,0},{2,3},{3,2},{4,5},{5,4},{6,7},{7,6},{8,9},{9,8},{10,11... | collective-permute-start | bytes 4718600 | tf_op jit(solution)/shard_map/ppermute | solution.py:105
Sparse Core Ops, SparseCore 0:
  10.6 66.1 all-gather.10
  78.4 62.1 all-gather.16
  142.2 62.1 all-gather.12
  215.0 36.8 all-gather.18
  253.3 35.9 all-gather.14

commit v2 on v1

v2 whole, which is shorter than its diff:
```python
import jax
import jax.numpy as jnp
from jax import lax
from jax.experimental import pallas as pl
from jax.experimental.pallas import tpu as pltpu
from jax.sharding import PartitionSpec as P

PARTS = (2, 2, 2, 1, 1)
AXES = ("row", "col")


def plain(panel, row_weights):
    total_rows = panel.shape[0] * lax.axis_size("row")
    weighted = row_weights[:, None] * panel
    partial_sum = jnp.dot(
        lax.all_gather(weighted, "col", axis=1, tiled=True).T,
        panel,
        preferred_element_type=jnp.float32,
        precision=lax.Precision.HIGHEST,
    )
    summed = lax.psum_scatter(partial_sum, "row", scatter_dimension=0, tiled=True)
    return summed * (1.0 / total_rows)


def product_body(where_ref, mine_ref, other_ref, high_ref, low_ref, *refs):
    out_ref, left_high, left_low = refs[-3:]
    k, e = where_ref[1], pl.program_id(0)
    m, width = mine_ref.shape[1], high_ref.shape[2]
    for side, ref in enumerate((mine_ref, other_ref)):
        x = ref[0]
        high = x.astype(jnp.bfloat16)
        left_high[side * m : (side + 1) * m] = high
        left_low[side * m : (side + 1) * m] = (x - high.astype(jnp.float32)).astype(jnp.bfloat16)

    def dot(a, b):
        return jnp.dot(a[...], b, preferred_element_type=jnp.float32)

    tile = min(256, width)
    for j in range(0, width, tile):
        high, low = high_ref[0, :, j : j + tile], low_ref[0, :, j : j + tile]
        total = dot(left_high, high) + (dot(left_high, low) + dot(left_low, high))
        for side, place in enumerate((k, 1 - k)):
            part = total[side * m : (side + 1) * m]
            before = out_ref[place, :, j : j + tile]
            out_ref[place, :, j : j + tile] = jnp.where(e == 0, part, before + part)


def product(where, mine, other, right, out, start):
    count, m, depth = mine.shape
    height = width = right[0].shape[2]
    assert start % m == 0
    left_spec = pl.BlockSpec((1, m, depth), lambda e, s: (s[0] ^ e, 0, 0))
    right_spec = pl.BlockSpec((1, depth, width), lambda e, s: (e, 0, 0))
    in_specs = [left_spec, left_spec, right_spec, right_spec]
    args = [where, mine, other, *right]
    aliases = {}
    if out is not None:
        in_specs.append(pl.BlockSpec(memory_space=pl.ANY))
        args.append(out)
        aliases = {len(args) - 1: 0}
    return pl.pallas_call(
        product_body,
        out_shape=jax.ShapeDtypeStruct((2, height, width), jnp.float32),
        grid_spec=pltpu.PrefetchScalarGridSpec(
            num_scalar_prefetch=1,
            grid=(count,),
            in_specs=in_specs,
            out_specs=pl.BlockSpec((2, m, width), lambda e, s: (0, start // m, 0)),
            scratch_shapes=[pltpu.VMEM((2 * m, depth), jnp.bfloat16)] * 2,
        ),
        input_output_aliases=aliases,
        compiler_params=pltpu.CompilerParams(vmem_limit_bytes=50 << 20),
        cost_estimate=pl.CostEstimate(
            flops=6 * 2 * m * width * depth * count,
            bytes_accessed=4 * (2 * count * m * depth + count * depth * width + 2 * m * width),
            transcendentals=0,
        ),
    )(*args)


def split(rights):
    whole = jnp.stack(rights)
    high = lax.reduce_precision(whole, 8, 7)
    return high.astype(jnp.bfloat16), (whole - high).astype(jnp.bfloat16)


def exchange(panel, row_weights):
    n = lax.axis_size("row")
    cols = lax.axis_size("col")
    r = lax.axis_index("row")
    k = lax.axis_index("col") % 2
    where = jnp.stack([r, k]).astype(jnp.int32)
    rows, width = panel.shape

    def across(x, e):
        moves = [(a * cols + b, (a ^ e) * cols + b) for a in range(n) for b in range(cols)]
        return lax.ppermute(x, AXES, moves)

    def swap(x):
        moves = [(a * cols + b, a * cols + (b ^ 1)) for a in range(n) for b in range(cols)]
        return lax.ppermute(x, AXES, moves)

    scale = jnp.sqrt(row_weights * (1.0 / (rows * n)))
    own = panel * scale[:, None]

    rights = [own]
    half = width // 2
    for e in range(1, n):
        top = 1 << (e.bit_length() - 1)
        low = e & -e
        if top == low:
            rights.append(across(own, e))
        else:
            parts = [across(rights[e ^ top][:, :half], top), across(rights[e ^ low][:, half:], low)]
            rights.append(jnp.concatenate(parts, axis=1))

    groups = [[b for b in range(cols) if b % 2 == core] for core in (0, 1)]
    unit = width // sum(PARTS)
    starts = [unit * sum(PARTS[:i]) for i in range(len(PARTS))]
    last = len(PARTS) - 1
    right = split(rights)
    outs, blocks = [None], []

    def finish(i):
        outs.append(product(where, blocks[i], swap(blocks[i]), right, outs[-1], starts[i]))

    for i, part in enumerate(PARTS):
        piece = lax.slice_in_dim(panel, starts[i], starts[i] + part * unit, axis=1).T * scale
        if i >= 2:
            piece, blocks[i - 2] = lax.optimization_barrier((piece, blocks[i - 2]))
        if i == 2:
            piece, rights[:3] = lax.optimization_barrier((piece, rights[:3]))
        if i == 3:
            piece, rights = lax.optimization_barrier((piece, rights))
        line = lax.all_gather(piece, "col", axis=0, axis_index_groups=groups)
        for done in {2: [0]}.get(i, []):
            finish(done)
            line, outs[-1] = lax.optimization_barrier((line, outs[-1]))
        block = lax.all_to_all(line, "row", 0, 0)
        for done in {3: [1, 2], 4: [3]}.get(i, []):
            finish(done)
            block, outs[-1] = lax.optimization_barrier((block, outs[-1]))
        blocks.append(block)
    finish(last)
    out = outs[-1]
    return out.reshape(2 * width, width)


def solution(mesh):
    n, cols = mesh.shape["row"], mesh.shape["col"]
    paired = cols == 2 * n and n & (n - 1) == 0 and n > 1
    return jax.shard_map(
        exchange if paired else plain,
        mesh=mesh,
        in_specs=(P("row", "col"), P("row")),
        out_specs=P("row", "col"),
        check_vma=False,
    )
```

time: 361 us -> 345 us (0.956)
  waiting for transfers between devices: 176 us -> 157 us
  other arithmetic: 8.41 us -> 19.2 us
  Pallas kernels: 70.5 us -> 65.5 us
    all_gather x5, waiting for transfers between devices: 105 us -> 93.4 us  [exchange(): line = lax.all_gather(piece, 'col', axis=0, axis_index_groups=groups)]
    convert_element_type x0 -> x1, other arithmetic: none -> 8.46 us  [split(): return (high.astype(jnp.bfloat16), (whole - high).astype(jnp.bfloat16))]
    all_to_all x4, waiting for transfers between devices: 53.5 us -> 47.2 us  [exchange(): block = lax.all_to_all(line, 'row', 0, 0)]
    pallas_call x5, Pallas kernels: 70.5 us -> 65.5 us  [product(): pl.pallas_call(product_body, out_shape=jax.ShapeDtypeStruct((2, height, w...]
    ppermute x4, waiting for transfers between devices: 16.9 us -> 12.1 us  [across(): return lax.ppermute(x, AXES, moves)]
  transfers between devices with their start and end apart: 18 -> 18, of which waited for: 9 -> 11; matrix products, arithmetic and copies ran while one was open for 8% -> 12% of each run, Pallas kernels for 17% -> 16%
where the time goes in v2:
time: 345 us; the launch traced here: 344 us
  waiting for transfers between devices  157 us (46%)
  Pallas kernels  65.5 us (19%)
  blocking collectives  40.6 us (12%)
  local copies, waits for them, and re-layouts  25.3 us (7%)
  starting transfers between devices  23.1 us (7%)
  other arithmetic  19.2 us (6%)
  between operations  13.2 us (4%)
    all_gather x5, waiting for transfers between devices, exchange(): line = lax.all_gather(piece, 'col', axis=0, axis_index_groups=groups)  93.4 us
    pallas_call x5, Pallas kernels, product(): pl.pallas_call(product_body, out_shape=jax.ShapeDtypeStruct((2, height, w...  65.5 us
    all_to_all x4, waiting for transfers between devices, exchange(): block = lax.all_to_all(line, 'row', 0, 0)  47.2 us
    all_to_all x1, blocking collectives, exchange(): block = lax.all_to_all(line, 'row', 0, 0)  40.6 us
    all_gather x5, local copies, waits for them, and re-layouts, exchange(): line = lax.all_gather(piece, 'col', axis=0, axis_index_groups=groups)  16.8 us
    all_to_all x4, starting transfers between devices, exchange(): block = lax.all_to_all(line, 'row', 0, 0)  16.7 us
    ppermute x4, waiting for transfers between devices, across(): return lax.ppermute(x, AXES, moves)  12.1 us
    convert_element_type x1, other arithmetic, split(): return (high.astype(jnp.bfloat16), (whole - high).astype(jnp.bfloat16))  8.46 us
  transfers between devices with their start and end apart: 18, of which 11 were waited for; matrix products, arithmetic and copies ran while one was open for 12% of the time, Pallas kernels for 16%

profile of v2, /device:TPU:0, one launch (start us, length us, event | category | flops | bytes accessed | tf_op | source)
XLA Modules:
  0.0 344.3 jit_solution(13921966760286948405)
XLA Ops:
  7.2 3.5 %multiply_bitcast_fusion = (f32[256,768]{0,1:T(8,128)}, f32[256,768]{0,1:T(8,128)}, f32[256,768]{0,1:T(8,128)}) fusion(f32[768,1024]{1,0:T(8,128)} %param.2, f32[768]{0:T(1024)S(1)} %multiply_sqrt_fusion), kind=kLoop, calls=%fused_computation.5 | loop fusion | flops 589824 | bytes 4721664 | tf_op jit(solution)/shard_map/mul | solution.py:128
  17.9 59.1 %all-gather.11.cloned.1.call-done = f32[1024,768]{0,1:T(8,128)} async-done(((f32[256,768]{0,1:T(8,128)}), f32[1024,768]{0,1:T(8,128)}) %all-gather.11.cloned.1.call-update) | async-done | bytes 3145744 | tf_op jit(solution)/shard_map/all_gather | solution.py:135
  77.0 3.6 %copy.7 = f32[1024,768]{1,0:T(8,128)} copy(f32[1024,768]{0,1:T(8,128)} %all-gather.11.cloned.1.call-done) | data formatting | bytes 6291456 | tf_op jit(solution)/shard_map/all_gather | solution.py:135
  80.6 40.6 %all_to_all.25.mine_ref = f32[4,256,768]{2,1,0:T(8,128)S(1)} all-to-all(f32[4,256,768]{2,1,0:T(8,128)} %bitcast.24), channel_id=1, replica_groups=mesh['row'=4,'col'=8] {'row'}, dimensions={0} | all-to-all | bytes 6291456 | tf_op jit(solution)/shard_map/all_to_all | solution.py:139
  128.4 12.4 %all-gather.17.cloned.1.call-done = f32[1024,768]{0,1:T(8,128)} async-done(((f32[256,768]{0,1:T(8,128)}), f32[1024,768]{0,1:T(8,128)}) %all-gather.17.cloned.1.call-update) | async-done | bytes 3145744 | tf_op jit(solution)/shard_map/all_gather | solution.py:135
  140.8 3.6 %copy.10 = f32[1024,768]{1,0:T(8,128)} copy(f32[1024,768]{0,1:T(8,128)} %all-gather.17.cloned.1.call-done) | data formatting | bytes 6291456 | tf_op jit(solution)/shard_map/all_gather | solution.py:135
  144.4 4.7 %all-to-all-start.3 = ((f32[4,256,768]{2,1,0:T(8,128)}), f32[4,256,768]{2,1,0:T(8,128)}, u32[]{:S(2)}, u32[]{:S(2)}) async-start(f32[4,256,768]{2,1,0:T(8,128)} %bitcast.23), calls=%async_computation.3 | async-start | bytes 6291456 | tf_op jit(solution)/shard_map/all_to_all | solution.py:139
  151.5 10.0 %collective-permute-done.3 = f32[768,512]{1,0:T(8,128)} collective-permute-done((f32[768,512]{1,0:T(8,128)}, f32[768,512]{1,0:T(8,128)}, u32[]{:S(2)}, u32[]{:S(2)}) %collective-permute-start.3) | collective-permute-done | bytes 1572896 | tf_op jit(solution)/shard_map/ppermute | solution.py:97
  166.8 8.5 %fusion = (bf16[4,768,1024]{2,1,0:T(8,128)(2,1)}, bf16[4,768,1024]{2,1,0:T(8,128)(2,1)}) fusion(f32[1,768,1024]{2,1,0:T(8,128)S(1)} %bitcast.25, f32[1,768,1024]{2,1,0:T(8,128)} %bitcast.9, f32[1,768,1024]{2,1,0:T(8,128)} %bitcast.8, f32[1,768,1024]{2,1,0:T(8,128)S(1)} %fusion.1), kind=kLoop, calls=%fused_computation.2 | loop fusion | flops 22020096 | bytes 25165824 | tf_op jit(solution)/shard_map/convert_element_type | solution.py:84
  175.2 15.1 %shard_map.28.refs_0_ = f32[2,1024,1024]{2,1,0:T(8,128)} custom-call(s32[2]{0:T(128)S(1)} %pad_add_fusion.where_ref, f32[4,256,768]{2,1,0:T(8,128)S(1)} %all_to_all.25.mine_ref, f32[4,256,768]{2,1,0:T(8,128)} %collective-permute-done.2.other_ref, bf16[4,768,1024]{2,1,0:T(8,128)(2,1)} %get-tuple-element.36.high_ref, ...), custom_call_target="tpu_custom_call" | custom-call | flops 9663676416 | bytes 20971520 | tf_op jit(solution)/shard_map/pallas_call | solution.py:61
  190.3 14.2 %all-gather.13.cloned.1.call-done = f32[1024,768]{0,1:T(8,128)} async-done(((f32[256,768]{0,1:T(8,128)}), f32[1024,768]{0,1:T(8,128)}) %all-gather.13.cloned.1.call-update) | async-done | bytes 3145744 | tf_op jit(solution)/shard_map/all_gather | solution.py:135
  204.6 3.6 %copy.8 = f32[1024,768]{1,0:T(8,128)} copy(f32[1024,768]{0,1:T(8,128)} %all-gather.13.cloned.1.call-done) | data formatting | bytes 6291456 | tf_op jit(solution)/shard_map/all_gather | solution.py:135
  208.2 4.7 %all-to-all-start.1 = ((f32[4,256,768]{2,1,0:T(8,128)}), f32[4,256,768]{2,1,0:T(8,128)}, u32[]{:S(2)}, u32[]{:S(2)}) async-start(f32[4,256,768]{2,1,0:T(8,128)} %bitcast.6), calls=%async_computation.1 | async-start | bytes 6291456 | tf_op jit(solution)/shard_map/all_to_all | solution.py:139
  215.1 34.2 %all-to-all-done.1.mine_ref = f32[4,256,768]{2,1,0:T(8,128)} async-done(((f32[4,256,768]{2,1,0:T(8,128)}), f32[4,256,768]{2,1,0:T(8,128)}, u32[]{:S(2)}, u32[]{:S(2)}) %all-to-all-start.1) | async-done | bytes 3145760 | tf_op jit(solution)/shard_map/all_to_all | solution.py:139
  255.2 3.7 %all-to-all-start.4 = ((f32[4,128,768]{2,1,0:T(8,128)}), f32[4,128,768]{2,1,0:T(8,128)S(1)}, u32[]{:S(2)}, u32[]{:S(2)}) async-start(f32[4,128,768]{2,1,0:T(8,128)} %bitcast.15), calls=%async_computation.4 | async-start | bytes 3145728 | tf_op jit(solution)/shard_map/all_to_all | solution.py:139
  259.5 15.3 %shard_map.29.refs_0_ = f32[2,1024,1024]{2,1,0:T(8,128)} custom-call(s32[2]{0:T(128)S(1)} %pad_add_fusion.where_ref, f32[4,256,768]{2,1,0:T(8,128)} %all-to-all-done.3.mine_ref, f32[4,256,768]{2,1,0:T(8,128)} %collective-permute-done.5.other_ref, bf16[4,768,1024]{2,1,0:T(8,128)(2,1)} %get-tuple-element.36.high_ref, ...), custom_call_target="tpu_custom_call", output_to_operand_aliasing={{}: (5, {})} | custom-call | flops 9663676416 | bytes 20971520 | tf_op jit(solution)/shard_map/pallas_call | solution.py:61
  274.8 3.6 %all-to-all-done.4.mine_ref = f32[4,128,768]{2,1,0:T(8,128)S(1)} async-done(((f32[4,128,768]{2,1,0:T(8,128)}), f32[4,128,768]{2,1,0:T(8,128)S(1)}, u32[]{:S(2)}, u32[]{:S(2)}) %all-to-all-start.4) | async-done | bytes 1572896 | tf_op jit(solution)/shard_map/all_to_all | solution.py:139
  278.4 15.3 %shard_map.30.refs_0_ = f32[2,1024,1024]{2,1,0:T(8,128)} custom-call(s32[2]{0:T(128)S(1)} %pad_add_fusion.where_ref, f32[4,256,768]{2,1,0:T(8,128)} %all-to-all-done.1.mine_ref, f32[4,256,768]{2,1,0:T(8,128)} %collective-permute-done.6.other_ref, bf16[4,768,1024]{2,1,0:T(8,128)(2,1)} %get-tuple-element.36.high_ref, ...), custom_call_target="tpu_custom_call", output_to_operand_aliasing={{}: (5, {})} | custom-call | flops 9663676416 | bytes 20971520 | tf_op jit(solution)/shard_map/pallas_call | solution.py:61
  293.7 4.7 %all-gather.15.cloned.1.call-done = f32[512,768]{0,1:T(8,128)} async-done(((f32[128,768]{0,1:T(8,128)}), f32[512,768]{0,1:T(8,128)}) %all-gather.15.cloned.1.call-update) | async-done | bytes 1572880 | tf_op jit(solution)/shard_map/all_gather | solution.py:135
  301.5 3.7 %all-to-all-start.2 = ((f32[4,128,768]{2,1,0:T(8,128)}), f32[4,128,768]{2,1,0:T(8,128)S(1)}, u32[]{:S(2)}, u32[]{:S(2)}) async-start(f32[4,128,768]{2,1,0:T(8,128)} %bitcast.26), calls=%async_computation.2 | async-start | bytes 3145728 | tf_op jit(solution)/shard_map/all_to_all | solution.py:139
  305.1 10.0 %shard_map.31.refs_0_ = f32[2,1024,1024]{2,1,0:T(8,128)} custom-call(s32[2]{0:T(128)S(1)} %pad_add_fusion.where_ref, f32[4,128,768]{2,1,0:T(8,128)S(1)} %all-to-all-done.4.mine_ref, f32[4,128,768]{2,1,0:T(8,128)} %collective-permute-done.7.other_ref, bf16[4,768,1024]{2,1,0:T(8,128)(2,1)} %get-tuple-element.36.high_ref, ...), custom_call_target="tpu_custom_call", output_to_operand_aliasing={{}: (5, {})} | custom-call | flops 4831838208 | bytes 16777216 | tf_op jit(solution)/shard_map/pallas_call | solution.py:61
  315.2 9.4 %all-to-all-done.2.mine_ref = f32[4,128,768]{2,1,0:T(8,128)S(1)} async-done(((f32[4,128,768]{2,1,0:T(8,128)}), f32[4,128,768]{2,1,0:T(8,128)S(1)}, u32[]{:S(2)}, u32[]{:S(2)}) %all-to-all-start.2) | async-done | bytes 1572896 | tf_op jit(solution)/shard_map/all_to_all | solution.py:139
  324.6 3.4 collective-permute-done.8.other_ref
  328.0 9.7 %shard_map.32 = f32[2,1024,1024]{2,1,0:T(8,128)} custom-call(s32[2]{0:T(128)S(1)} %pad_add_fusion.where_ref, f32[4,128,768]{2,1,0:T(8,128)S(1)} %all-to-all-done.2.mine_ref, f32[4,128,768]{2,1,0:T(8,128)S(1)} %collective-permute-done.8.other_ref, bf16[4,768,1024]{2,1,0:T(8,128)(2,1)} %get-tuple-element.36.high_ref, ...), custom_call_target="tpu_custom_call", output_to_operand_aliasing={{}: (5, {})} | custom-call | flops 4831838208 | bytes 16777216 | tf_op jit(solution)/shard_map/pallas_call | solution.py:61
  (41 shorter events, 34.6 us)
Async XLA Ops:
  6.5 70.5 %all-gather.11.cloned.1.call-start = ((), (), s32[]{:S(2)}) async-start(), calls=%async_computation.5 | async-start | bytes 3932160 | tf_op jit(solution)/shard_map/all_gather | solution.py:135
  7.2 4.3 %copy-start = (f32[768,1024]{1,0:T(8,128)S(1)}, f32[768,1024]{1,0:T(8,128)}, u32[]{:S(2)}) copy-start(f32[768,1024]{1,0:T(8,128)} %param.2) | copy-start | bytes 9437188
  10.7 130.1 %all-gather.17.cloned.1.call-start = ((), (), s32[]{:S(2)}) async-start(), calls=%async_computation.8 | async-start | bytes 3932160 | tf_op jit(solution)/shard_map/all_gather | solution.py:135
  11.5 193.1 %all-gather.13.cloned.1.call-start = ((), (), s32[]{:S(2)}) async-start(), calls=%async_computation.6 | async-start | bytes 3932160 | tf_op jit(solution)/shard_map/all_gather | solution.py:135
  13.5 107.7 %collective-permute-start.1 = (f32[768,1024]{1,0:T(8,128)}, f32[768,1024]{1,0:T(8,128)}, u32[]{:S(2)}, u32[]{:S(2)}) collective-permute-start(f32[768,1024]{1,0:T(8,128)} %broadcast_multiply_fusion), channel_id=1, source_target_pairs={{0,16},{1,17},{2,18},{3,19},{4,20},{5,21},{6,22},{7,23},{8,24},{9,... | collective-permute-start | bytes 9437192 | tf_op jit(solution)/shard_map/ppermute | solution.py:97
  16.4 104.8 %collective-permute-start = (f32[768,1024]{1,0:T(8,128)}, f32[768,1024]{1,0:T(8,128)}, u32[]{:S(2)}, u32[]{:S(2)}) collective-permute-start(f32[768,1024]{1,0:T(8,128)} %broadcast_multiply_fusion), channel_id=1, source_target_pairs={{0,8},{1,9},{2,10},{3,11},{4,12},{5,13},{6,14},{7,15},{8,0},{9,1},... | collective-permute-start | bytes 9437192 | tf_op jit(solution)/shard_map/ppermute | solution.py:97
  121.2 54.0 %collective-permute-start.2 = (f32[4,256,768]{2,1,0:T(8,128)S(1)}, f32[4,256,768]{2,1,0:T(8,128)}, u32[]{:S(2)}, u32[]{:S(2)}) collective-permute-start(f32[4,256,768]{2,1,0:T(8,128)S(1)} %all_to_all.25.mine_ref), channel_id=1, source_target_pairs={{0,1},{1,0},{2,3},{3,2},{4,5},{5,4},{6,7},{7,6},{8,9},{9,8},{10,11... | collective-permute-start | bytes 9437192 | tf_op jit(solution)/shard_map/ppermute | solution.py:101
  124.0 37.5 %collective-permute-start.3 = (f32[768,512]{1,0:T(8,128)}, f32[768,512]{1,0:T(8,128)}, u32[]{:S(2)}, u32[]{:S(2)}) collective-permute-start(f32[768,512]{1,0:T(8,128)} %slice.28), channel_id=1, source_target_pairs={{0,16},{1,17},{2,18},{3,19},{4,20},{5,21},{6,22},{7,23},{8,24},{9,... | collective-permute-start | bytes 4718600 | tf_op jit(solution)/shard_map/ppermute | solution.py:97
  127.7 37.5 %collective-permute-start.4 = (f32[768,512]{1,0:T(8,128)}, f32[768,512]{1,0:T(8,128)}, u32[]{:S(2)}, u32[]{:S(2)}) collective-permute-start(f32[768,512]{1,0:T(8,128)} %slice.29), channel_id=1, source_target_pairs={{0,8},{1,9},{2,10},{3,11},{4,12},{5,13},{6,14},{7,15},{8,0},{9,1},... | collective-permute-start | bytes 4718600 | tf_op jit(solution)/shard_map/ppermute | solution.py:97
  144.4 63.8 %all-to-all-start.3 = ((f32[4,256,768]{2,1,0:T(8,128)}), f32[4,256,768]{2,1,0:T(8,128)}, u32[]{:S(2)}, u32[]{:S(2)}) async-start(f32[4,256,768]{2,1,0:T(8,128)} %bitcast.23), calls=%async_computation.3 | async-start | bytes 6291456 | tf_op jit(solution)/shard_map/all_to_all | solution.py:139
  208.2 41.1 %all-to-all-start.1 = ((f32[4,256,768]{2,1,0:T(8,128)}), f32[4,256,768]{2,1,0:T(8,128)}, u32[]{:S(2)}, u32[]{:S(2)}) async-start(f32[4,256,768]{2,1,0:T(8,128)} %bitcast.6), calls=%async_computation.1 | async-start | bytes 6291456 | tf_op jit(solution)/shard_map/all_to_all | solution.py:139
  212.8 39.4 %all-gather.19.cloned.1.call-start = ((), (), s32[]{:S(2)}) async-start(), calls=%async_computation.9 | async-start | bytes 1966080 | tf_op jit(solution)/shard_map/all_gather | solution.py:135
  215.0 44.5 %collective-permute-start.5 = (f32[4,256,768]{2,1,0:T(8,128)}, f32[4,256,768]{2,1,0:T(8,128)}, u32[]{:S(2)}, u32[]{:S(2)}) collective-permute-start(f32[4,256,768]{2,1,0:T(8,128)} %all-to-all-done.3.mine_ref), channel_id=1, source_target_pairs={{0,1},{1,0},{2,3},{3,2},{4,5},{5,4},{6,7},{7,6},{8,9},{9,8},{10,11... | collective-permute-start | bytes 9437192 | tf_op jit(solution)/shard_map/ppermute | solution.py:101
  249.3 29.1 %collective-permute-start.6 = (f32[4,256,768]{2,1,0:T(8,128)}, f32[4,256,768]{2,1,0:T(8,128)}, u32[]{:S(2)}, u32[]{:S(2)}) collective-permute-start(f32[4,256,768]{2,1,0:T(8,128)} %all-to-all-done.1.mine_ref), channel_id=1, source_target_pairs={{0,1},{1,0},{2,3},{3,2},{4,5},{5,4},{6,7},{7,6},{8,9},{9,8},{10,11... | collective-permute-start | bytes 9437192 | tf_op jit(solution)/shard_map/ppermute | solution.py:101
  255.2 23.2 %all-to-all-start.4 = ((f32[4,128,768]{2,1,0:T(8,128)}), f32[4,128,768]{2,1,0:T(8,128)S(1)}, u32[]{:S(2)}, u32[]{:S(2)}) async-start(f32[4,128,768]{2,1,0:T(8,128)} %bitcast.15), calls=%async_computation.4 | async-start | bytes 3145728 | tf_op jit(solution)/shard_map/all_to_all | solution.py:139
  258.9 39.5 %all-gather.15.cloned.1.call-start = ((), (), s32[]{:S(2)}) async-start(), calls=%async_computation.7 | async-start | bytes 1966080 | tf_op jit(solution)/shard_map/all_gather | solution.py:135
  293.7 11.4 %collective-permute-start.7 = (f32[4,128,768]{2,1,0:T(8,128)S(1)}, f32[4,128,768]{2,1,0:T(8,128)}, u32[]{:S(2)}, u32[]{:S(2)}) collective-permute-start(f32[4,128,768]{2,1,0:T(8,128)S(1)} %all-to-all-done.4.mine_ref), channel_id=1, source_target_pairs={{0,1},{1,0},{2,3},{3,2},{4,5},{5,4},{6,7},{7,6},{8,9},{9,8},{10,11... | collective-permute-start | bytes 4718600 | tf_op jit(solution)/shard_map/ppermute | solution.py:101
  301.5 23.2 %all-to-all-start.2 = ((f32[4,128,768]{2,1,0:T(8,128)}), f32[4,128,768]{2,1,0:T(8,128)S(1)}, u32[]{:S(2)}, u32[]{:S(2)}) async-start(f32[4,128,768]{2,1,0:T(8,128)} %bitcast.26), calls=%async_computation.2 | async-start | bytes 3145728 | tf_op jit(solution)/shard_map/all_to_all | solution.py:139
  324.6 3.4 collective-permute-start.8
Sparse Core Ops, SparseCore 0:
  10.8 66.1 all-gather.10
  78.6 62.1 all-gather.16
  142.4 62.1 all-gather.12
  215.2 36.9 all-gather.18
  261.0 37.3 all-gather.14

commit v3 on v2

--- a/solution.py
+++ b/solution.py
@@ -70,11 +70,7 @@
         ),
         input_output_aliases=aliases,
         compiler_params=pltpu.CompilerParams(vmem_limit_bytes=50 << 20),
-        cost_estimate=pl.CostEstimate(
-            flops=6 * 2 * m * width * depth * count,
-            bytes_accessed=4 * (2 * count * m * depth + count * depth * width + 2 * m * width),
-            transcendentals=0,
-        ),
+        cost_estimate=pl.CostEstimate(flops=4 * m * width * depth, bytes_accessed=8 * m * width, transcendentals=0),
     )(*args)
 
 

time: 345 us -> 342 us (level)
    all_gather x5, waiting for transfers between devices: 93.4 us -> 89.2 us  [exchange(): line = lax.all_gather(piece, 'col', axis=0, axis_index_groups=groups)]
  transfers between devices with their start and end apart: 18 -> 18, of which waited for: 11 -> 10; matrix products, arithmetic and copies ran while one was open for 12% -> 11% of each run, Pallas kernels for 16% -> 16%
where the time goes in v3:
time: 342 us; the launch traced here: 341 us
  waiting for transfers between devices  154 us (45%)
  Pallas kernels  65.6 us (19%)
  blocking collectives  40.6 us (12%)
  local copies, waits for them, and re-layouts  24.1 us (7%)
  starting transfers between devices  24 us (7%)
  other arithmetic  19.2 us (6%)
  between operations  13.3 us (4%)
    all_gather x5, waiting for transfers between devices, exchange(): line = lax.all_gather(piece, 'col', axis=0, axis_index_groups=groups)  89.2 us
    pallas_call x5, Pallas kernels, product(): pl.pallas_call(product_body, out_shape=jax.ShapeDtypeStruct((2, height, w...  65.6 us
    all_to_all x4, waiting for transfers between devices, exchange(): block = lax.all_to_all(line, 'row', 0, 0)  48.6 us
    all_to_all x1, blocking collectives, exchange(): block = lax.all_to_all(line, 'row', 0, 0)  40.6 us
    all_to_all x4, starting transfers between devices, exchange(): block = lax.all_to_all(line, 'row', 0, 0)  16.3 us
    all_gather x5, local copies, waits for them, and re-layouts, exchange(): line = lax.all_gather(piece, 'col', axis=0, axis_index_groups=groups)  15.5 us
    ppermute x4, waiting for transfers between devices, across(): return lax.ppermute(x, AXES, moves)  12.1 us
    convert_element_type x1, other arithmetic, split(): return (high.astype(jnp.bfloat16), (whole - high).astype(jnp.bfloat16))  8.44 us
  transfers between devices with their start and end apart: 18, of which 10 were waited for; matrix products, arithmetic and copies ran while one was open for 11% of the time, Pallas kernels for 16%

profile of v3, /device:TPU:0, one launch (start us, length us, event | category | flops | bytes accessed | tf_op | source)
XLA Modules:
  0.0 340.9 jit_solution(14819486905947367389)
XLA Ops:
  7.2 3.5 %multiply_bitcast_fusion = (f32[256,768]{0,1:T(8,128)}, f32[256,768]{0,1:T(8,128)}, f32[256,768]{0,1:T(8,128)}) fusion(f32[768,1024]{1,0:T(8,128)} %param.2, f32[768]{0:T(1024)S(1)} %multiply_sqrt_fusion), kind=kLoop, calls=%fused_computation.5 | loop fusion | flops 589824 | bytes 4721664 | tf_op jit(solution)/shard_map/mul | solution.py:124
  17.9 59.1 %all-gather.11.cloned.1.call-done = f32[1024,768]{0,1:T(8,128)} async-done(((f32[256,768]{0,1:T(8,128)}), f32[1024,768]{0,1:T(8,128)}) %all-gather.11.cloned.1.call-update) | async-done | bytes 3145744 | tf_op jit(solution)/shard_map/all_gather | solution.py:131
  79.4 40.6 %all_to_all.25.mine_ref = f32[4,256,768]{2,1,0:T(8,128)} all-to-all(f32[4,256,768]{2,1,0:T(8,128)S(1)} %bitcast.25), channel_id=1, replica_groups=mesh['row'=4,'col'=8] {'row'}, dimensions={0} | all-to-all | bytes 6291456 | tf_op jit(solution)/shard_map/all_to_all | solution.py:135
  128.5 12.3 %all-gather.17.cloned.1.call-done = f32[1024,768]{0,1:T(8,128)} async-done(((f32[256,768]{0,1:T(8,128)}), f32[1024,768]{0,1:T(8,128)}) %all-gather.17.cloned.1.call-update) | async-done | bytes 3145744 | tf_op jit(solution)/shard_map/all_gather | solution.py:131
  140.8 3.6 %copy.10 = f32[1024,768]{1,0:T(8,128)} copy(f32[1024,768]{0,1:T(8,128)} %all-gather.17.cloned.1.call-done) | data formatting | bytes 6291456 | tf_op jit(solution)/shard_map/all_gather | solution.py:131
  144.4 3.7 %all-to-all-start.3 = ((f32[4,256,768]{2,1,0:T(8,128)}), f32[4,256,768]{2,1,0:T(8,128)S(1)}, u32[]{:S(2)}, u32[]{:S(2)}) async-start(f32[4,256,768]{2,1,0:T(8,128)} %bitcast.23), calls=%async_computation.3 | async-start | bytes 6291456 | tf_op jit(solution)/shard_map/all_to_all | solution.py:135
  150.5 9.8 %collective-permute-done.3 = f32[768,512]{1,0:T(8,128)} collective-permute-done((f32[768,512]{1,0:T(8,128)}, f32[768,512]{1,0:T(8,128)}, u32[]{:S(2)}, u32[]{:S(2)}) %collective-permute-start.3) | collective-permute-done | bytes 1572896 | tf_op jit(solution)/shard_map/ppermute | solution.py:93
  165.8 8.4 %fusion = (bf16[4,768,1024]{2,1,0:T(8,128)(2,1)}, bf16[4,768,1024]{2,1,0:T(8,128)(2,1)}) fusion(f32[1,768,1024]{2,1,0:T(8,128)S(1)} %bitcast.26, f32[1,768,1024]{2,1,0:T(8,128)} %bitcast.9, f32[1,768,1024]{2,1,0:T(8,128)} %bitcast.8, f32[1,768,1024]{2,1,0:T(8,128)S(1)} %fusion.1), kind=kLoop, calls=%fused_computation.2 | loop fusion | flops 22020096 | bytes 25165824 | tf_op jit(solution)/shard_map/convert_element_type | solution.py:80
  174.2 15.4 %shard_map.28.refs_0_ = f32[2,1024,1024]{2,1,0:T(8,128)} custom-call(s32[2]{0:T(128)S(1)} %pad_add_fusion.where_ref, f32[4,256,768]{2,1,0:T(8,128)} %all_to_all.25.mine_ref, f32[4,256,768]{2,1,0:T(8,128)} %collective-permute-done.2.other_ref, bf16[4,768,1024]{2,1,0:T(8,128)(2,1)} %get-tuple-element.36.high_ref, bf16[4,768,1024]{2,1,0:T(8,128)(2,1)} %get-tuple-element.35.low_ref), custom_call_target="tpu_custom_call" | custom-call | flops 805306368 | bytes 2097152 | tf_op jit(solution)/shard_map/pallas_call | solution.py:61
  189.6 15.0 %all-gather.13.cloned.1.call-done = f32[1024,768]{0,1:T(8,128)} async-done(((f32[256,768]{0,1:T(8,128)}), f32[1024,768]{0,1:T(8,128)}) %all-gather.13.cloned.1.call-update) | async-done | bytes 3145744 | tf_op jit(solution)/shard_map/all_gather | solution.py:131
  204.6 3.5 %copy.8 = f32[1024,768]{1,0:T(8,128)} copy(f32[1024,768]{0,1:T(8,128)} %all-gather.13.cloned.1.call-done) | data formatting | bytes 6291456 | tf_op jit(solution)/shard_map/all_gather | solution.py:131
  208.1 4.7 %all-to-all-start.1 = ((f32[4,256,768]{2,1,0:T(8,128)}), f32[4,256,768]{2,1,0:T(8,128)}, u32[]{:S(2)}, u32[]{:S(2)}) async-start(f32[4,256,768]{2,1,0:T(8,128)} %bitcast.24), calls=%async_computation.1 | async-start | bytes 6291456 | tf_op jit(solution)/shard_map/all_to_all | solution.py:135
  215.2 34.0 %all-to-all-done.1.mine_ref = f32[4,256,768]{2,1,0:T(8,128)} async-done(((f32[4,256,768]{2,1,0:T(8,128)}), f32[4,256,768]{2,1,0:T(8,128)}, u32[]{:S(2)}, u32[]{:S(2)}) %all-to-all-start.1) | async-done | bytes 3145760 | tf_op jit(solution)/shard_map/all_to_all | solution.py:135
  252.1 3.0 copy.11
  255.1 4.3 %all-to-all-start.4 = ((f32[4,128,768]{2,1,0:T(8,128)}), f32[4,128,768]{2,1,0:T(8,128)}, u32[]{:S(2)}, u32[]{:S(2)}) async-start(f32[4,128,768]{2,1,0:T(8,128)} %bitcast.27), calls=%async_computation.4 | async-start | bytes 3145728 | tf_op jit(solution)/shard_map/all_to_all | solution.py:135
  259.5 15.1 %shard_map.29.refs_0_ = f32[2,1024,1024]{2,1,0:T(8,128)} custom-call(s32[2]{0:T(128)S(1)} %pad_add_fusion.where_ref, f32[4,256,768]{2,1,0:T(8,128)S(1)} %all-to-all-done.3.mine_ref, f32[4,256,768]{2,1,0:T(8,128)} %collective-permute-done.5.other_ref, bf16[4,768,1024]{2,1,0:T(8,128)(2,1)} %get-tuple-element.36.high_ref, ...), custom_call_target="tpu_custom_call", output_to_operand_aliasing={{}: (5, {})} | custom-call | flops 805306368 | bytes 2097152 | tf_op jit(solution)/shard_map/pallas_call | solution.py:61
  274.6 4.5 %all-to-all-done.4.mine_ref = f32[4,128,768]{2,1,0:T(8,128)} async-done(((f32[4,128,768]{2,1,0:T(8,128)}), f32[4,128,768]{2,1,0:T(8,128)}, u32[]{:S(2)}, u32[]{:S(2)}) %all-to-all-start.4) | async-done | bytes 1572896 | tf_op jit(solution)/shard_map/all_to_all | solution.py:135
  279.1 15.3 %shard_map.30.refs_0_ = f32[2,1024,1024]{2,1,0:T(8,128)} custom-call(s32[2]{0:T(128)S(1)} %pad_add_fusion.where_ref, f32[4,256,768]{2,1,0:T(8,128)} %all-to-all-done.1.mine_ref, f32[4,256,768]{2,1,0:T(8,128)} %collective-permute-done.6.other_ref, bf16[4,768,1024]{2,1,0:T(8,128)(2,1)} %get-tuple-element.36.high_ref, ...), custom_call_target="tpu_custom_call", output_to_operand_aliasing={{}: (5, {})} | custom-call | flops 805306368 | bytes 2097152 | tf_op jit(solution)/shard_map/pallas_call | solution.py:61
  294.4 3.0 copy.9
  297.5 3.6 %all-to-all-start.2 = ((f32[4,128,768]{2,1,0:T(8,128)}), f32[4,128,768]{2,1,0:T(8,128)S(1)}, u32[]{:S(2)}, u32[]{:S(2)}) async-start(f32[4,128,768]{2,1,0:T(8,128)} %bitcast.28), calls=%async_computation.2 | async-start | bytes 3145728 | tf_op jit(solution)/shard_map/all_to_all | solution.py:135
  301.0 10.0 %shard_map.31.refs_0_ = f32[2,1024,1024]{2,1,0:T(8,128)} custom-call(s32[2]{0:T(128)S(1)} %pad_add_fusion.where_ref, f32[4,128,768]{2,1,0:T(8,128)} %all-to-all-done.4.mine_ref, f32[4,128,768]{2,1,0:T(8,128)S(1)} %collective-permute-done.7.other_ref, bf16[4,768,1024]{2,1,0:T(8,128)(2,1)} %get-tuple-element.36.high_ref, ...), custom_call_target="tpu_custom_call", output_to_operand_aliasing={{}: (5, {})} | custom-call | flops 402653184 | bytes 1048576 | tf_op jit(solution)/shard_map/pallas_call | solution.py:61
  311.0 10.1 %all-to-all-done.2.mine_ref = f32[4,128,768]{2,1,0:T(8,128)S(1)} async-done(((f32[4,128,768]{2,1,0:T(8,128)}), f32[4,128,768]{2,1,0:T(8,128)S(1)}, u32[]{:S(2)}, u32[]{:S(2)}) %all-to-all-start.2) | async-done | bytes 1572896 | tf_op jit(solution)/shard_map/all_to_all | solution.py:135
  321.2 3.4 collective-permute-done.8.other_ref
  324.6 9.7 %shard_map.32 = f32[2,1024,1024]{2,1,0:T(8,128)} custom-call(s32[2]{0:T(128)S(1)} %pad_add_fusion.where_ref, f32[4,128,768]{2,1,0:T(8,128)S(1)} %all-to-all-done.2.mine_ref, f32[4,128,768]{2,1,0:T(8,128)S(1)} %collective-permute-done.8.other_ref, bf16[4,768,1024]{2,1,0:T(8,128)(2,1)} %get-tuple-element.36.high_ref, ...), custom_call_target="tpu_custom_call", output_to_operand_aliasing={{}: (5, {})} | custom-call | flops 402653184 | bytes 1048576 | tf_op jit(solution)/shard_map/pallas_call | solution.py:61
  (41 shorter events, 31.9 us)
Async XLA Ops:
  6.5 70.5 %all-gather.11.cloned.1.call-start = ((), (), s32[]{:S(2)}) async-start(), calls=%async_computation.5 | async-start | bytes 3932160 | tf_op jit(solution)/shard_map/all_gather | solution.py:131
  7.2 4.3 %copy-start = (f32[768,1024]{1,0:T(8,128)S(1)}, f32[768,1024]{1,0:T(8,128)}, u32[]{:S(2)}) copy-start(f32[768,1024]{1,0:T(8,128)} %param.2) | copy-start | bytes 9437188
  10.7 130.1 %all-gather.17.cloned.1.call-start = ((), (), s32[]{:S(2)}) async-start(), calls=%async_computation.8 | async-start | bytes 3932160 | tf_op jit(solution)/shard_map/all_gather | solution.py:131
  11.5 193.1 %all-gather.13.cloned.1.call-start = ((), (), s32[]{:S(2)}) async-start(), calls=%async_computation.6 | async-start | bytes 3932160 | tf_op jit(solution)/shard_map/all_gather | solution.py:131
  13.5 106.6 %collective-permute-start.1 = (f32[768,1024]{1,0:T(8,128)}, f32[768,1024]{1,0:T(8,128)}, u32[]{:S(2)}, u32[]{:S(2)}) collective-permute-start(f32[768,1024]{1,0:T(8,128)} %broadcast_multiply_fusion), channel_id=1, source_target_pairs={{0,16},{1,17},{2,18},{3,19},{4,20},{5,21},{6,22},{7,23},{8,24},{9,... | collective-permute-start | bytes 9437192 | tf_op jit(solution)/shard_map/ppermute | solution.py:93
  16.4 103.6 %collective-permute-start = (f32[768,1024]{1,0:T(8,128)}, f32[768,1024]{1,0:T(8,128)}, u32[]{:S(2)}, u32[]{:S(2)}) collective-permute-start(f32[768,1024]{1,0:T(8,128)} %broadcast_multiply_fusion), channel_id=1, source_target_pairs={{0,8},{1,9},{2,10},{3,11},{4,12},{5,13},{6,14},{7,15},{8,0},{9,1},... | collective-permute-start | bytes 9437192 | tf_op jit(solution)/shard_map/ppermute | solution.py:93
  120.1 54.2 %collective-permute-start.2 = (f32[4,256,768]{2,1,0:T(8,128)}, f32[4,256,768]{2,1,0:T(8,128)}, u32[]{:S(2)}, u32[]{:S(2)}) collective-permute-start(f32[4,256,768]{2,1,0:T(8,128)} %all_to_all.25.mine_ref), channel_id=1, source_target_pairs={{0,1},{1,0},{2,3},{3,2},{4,5},{5,4},{6,7},{7,6},{8,9},{9,8},{10,11... | collective-permute-start | bytes 9437192 | tf_op jit(solution)/shard_map/ppermute | solution.py:97
  122.8 37.5 %collective-permute-start.3 = (f32[768,512]{1,0:T(8,128)}, f32[768,512]{1,0:T(8,128)}, u32[]{:S(2)}, u32[]{:S(2)}) collective-permute-start(f32[768,512]{1,0:T(8,128)} %slice.28), channel_id=1, source_target_pairs={{0,16},{1,17},{2,18},{3,19},{4,20},{5,21},{6,22},{7,23},{8,24},{9,... | collective-permute-start | bytes 4718600 | tf_op jit(solution)/shard_map/ppermute | solution.py:93
  126.7 37.5 %collective-permute-start.4 = (f32[768,512]{1,0:T(8,128)}, f32[768,512]{1,0:T(8,128)}, u32[]{:S(2)}, u32[]{:S(2)}) collective-permute-start(f32[768,512]{1,0:T(8,128)} %slice.29), channel_id=1, source_target_pairs={{0,8},{1,9},{2,10},{3,11},{4,12},{5,13},{6,14},{7,15},{8,0},{9,1},... | collective-permute-start | bytes 4718600 | tf_op jit(solution)/shard_map/ppermute | solution.py:93
  144.4 63.7 %all-to-all-start.3 = ((f32[4,256,768]{2,1,0:T(8,128)}), f32[4,256,768]{2,1,0:T(8,128)S(1)}, u32[]{:S(2)}, u32[]{:S(2)}) async-start(f32[4,256,768]{2,1,0:T(8,128)} %bitcast.23), calls=%async_computation.3 | async-start | bytes 6291456 | tf_op jit(solution)/shard_map/all_to_all | solution.py:135
  208.1 41.1 %all-to-all-start.1 = ((f32[4,256,768]{2,1,0:T(8,128)}), f32[4,256,768]{2,1,0:T(8,128)}, u32[]{:S(2)}, u32[]{:S(2)}) async-start(f32[4,256,768]{2,1,0:T(8,128)} %bitcast.24), calls=%async_computation.1 | async-start | bytes 6291456 | tf_op jit(solution)/shard_map/all_to_all | solution.py:135
  212.8 39.3 %all-gather.19.cloned.1.call-start = ((), (), s32[]{:S(2)}) async-start(), calls=%async_computation.9 | async-start | bytes 1966080 | tf_op jit(solution)/shard_map/all_gather | solution.py:131
  215.1 79.4 %all-gather.15.cloned.1.call-start = ((), (), s32[]{:S(2)}) async-start(), calls=%async_computation.7 | async-start | bytes 1966080 | tf_op jit(solution)/shard_map/all_gather | solution.py:131
  215.1 44.3 %collective-permute-start.5 = (f32[4,256,768]{2,1,0:T(8,128)S(1)}, f32[4,256,768]{2,1,0:T(8,128)}, u32[]{:S(2)}, u32[]{:S(2)}) collective-permute-start(f32[4,256,768]{2,1,0:T(8,128)S(1)} %all-to-all-done.3.mine_ref), channel_id=1, source_target_pairs={{0,1},{1,0},{2,3},{3,2},{4,5},{5,4},{6,7},{7,6},{8,9},{9,8},{10,11... | collective-permute-start | bytes 9437192 | tf_op jit(solution)/shard_map/ppermute | solution.py:97
  249.2 29.9 %collective-permute-start.6 = (f32[4,256,768]{2,1,0:T(8,128)}, f32[4,256,768]{2,1,0:T(8,128)}, u32[]{:S(2)}, u32[]{:S(2)}) collective-permute-start(f32[4,256,768]{2,1,0:T(8,128)} %all-to-all-done.1.mine_ref), channel_id=1, source_target_pairs={{0,1},{1,0},{2,3},{3,2},{4,5},{5,4},{6,7},{7,6},{8,9},{9,8},{10,11... | collective-permute-start | bytes 9437192 | tf_op jit(solution)/shard_map/ppermute | solution.py:97
  255.1 24.0 %all-to-all-start.4 = ((f32[4,128,768]{2,1,0:T(8,128)}), f32[4,128,768]{2,1,0:T(8,128)}, u32[]{:S(2)}, u32[]{:S(2)}) async-start(f32[4,128,768]{2,1,0:T(8,128)} %bitcast.27), calls=%async_computation.4 | async-start | bytes 3145728 | tf_op jit(solution)/shard_map/all_to_all | solution.py:135
  294.4 6.6 %collective-permute-start.7 = (f32[4,128,768]{2,1,0:T(8,128)}, f32[4,128,768]{2,1,0:T(8,128)S(1)}, u32[]{:S(2)}, u32[]{:S(2)}) collective-permute-start(f32[4,128,768]{2,1,0:T(8,128)} %all-to-all-done.4.mine_ref), channel_id=1, source_target_pairs={{0,1},{1,0},{2,3},{3,2},{4,5},{5,4},{6,7},{7,6},{8,9},{9,8},{10,11... | collective-permute-start | bytes 4718600 | tf_op jit(solution)/shard_map/ppermute | solution.py:97
  297.5 23.7 %all-to-all-start.2 = ((f32[4,128,768]{2,1,0:T(8,128)}), f32[4,128,768]{2,1,0:T(8,128)S(1)}, u32[]{:S(2)}, u32[]{:S(2)}) async-start(f32[4,128,768]{2,1,0:T(8,128)} %bitcast.28), calls=%async_computation.2 | async-start | bytes 3145728 | tf_op jit(solution)/shard_map/all_to_all | solution.py:135
  321.2 3.4 %collective-permute-start.8 = (f32[4,128,768]{2,1,0:T(8,128)S(1)}, f32[4,128,768]{2,1,0:T(8,128)S(1)}, u32[]{:S(2)}, u32[]{:S(2)}) collective-permute-start(f32[4,128,768]{2,1,0:T(8,128)S(1)} %all-to-all-done.2.mine_ref), channel_id=1, source_target_pairs={{0,1},{1,0},{2,3},{3,2},{4,5},{5,4},{6,7},{7,6},{8,9},{9,8},{10,11... | collective-permute-start | bytes 4718600 | tf_op jit(solution)/shard_map/ppermute | solution.py:97
Sparse Core Ops, SparseCore 0:
  10.8 66.1 all-gather.10
  78.6 62.1 all-gather.16
  142.4 62.1 all-gather.12
  215.2 36.8 all-gather.18
  253.5 35.9 all-gather.14

commit v4 on v3

--- a/solution.py
+++ b/solution.py
@@ -5,7 +5,7 @@
 from jax.experimental.pallas import tpu as pltpu
 from jax.sharding import PartitionSpec as P
 
-PARTS = (2, 2, 2, 1, 1)
+PARTS = ((4, 2), (0, 3), (6, 2), (3, 1))
 AXES = ("row", "col")
 
 
@@ -111,8 +111,8 @@
             rights.append(jnp.concatenate(parts, axis=1))
 
     groups = [[b for b in range(cols) if b % 2 == core] for core in (0, 1)]
-    unit = width // sum(PARTS)
-    starts = [unit * sum(PARTS[:i]) for i in range(len(PARTS))]
+    unit = width // sum(part for _, part in PARTS)
+    starts = [start * unit for start, _ in PARTS]
     last = len(PARTS) - 1
     right = split(rights)
     outs, blocks = [None], []
@@ -120,7 +120,7 @@
     def finish(i):
         outs.append(product(where, blocks[i], swap(blocks[i]), right, outs[-1], starts[i]))
 
-    for i, part in enumerate(PARTS):
+    for i, (_, part) in enumerate(PARTS):
         piece = lax.slice_in_dim(panel, starts[i], starts[i] + part * unit, axis=1).T * scale
         if i >= 2:
             piece, blocks[i - 2] = lax.optimization_barrier((piece, blocks[i - 2]))
@@ -133,7 +133,7 @@
             finish(done)
             line, outs[-1] = lax.optimization_barrier((line, outs[-1]))
         block = lax.all_to_all(line, "row", 0, 0)
-        for done in {3: [1, 2], 4: [3]}.get(i, []):
+        for done in {2: [1], 3: [2]}.get(i, []):
             finish(done)
             block, outs[-1] = lax.optimization_barrier((block, outs[-1]))
         blocks.append(block)

time: 342 us -> 393 us (1.15)
  waiting for transfers between devices: 154 us -> 248 us
  blocking collectives: 40.6 us -> 0 us
    all_gather x5 -> x4, waiting for transfers between devices: 89.2 us -> 142 us  [exchange(): line = lax.all_gather(piece, 'col', axis=0, axis_index_groups=groups)]
    all_to_all x1 -> x0, blocking collectives: 40.6 us -> none  [exchange(): block = lax.all_to_all(line, 'row', 0, 0)]
    ppermute x4, waiting for transfers between devices: 12.1 us -> 42.7 us  [across(): return lax.ppermute(x, AXES, moves)]
    all_to_all x4, waiting for transfers between devices: 48.6 us -> 59.7 us  [exchange(): block = lax.all_to_all(line, 'row', 0, 0)]
    pallas_call x5 -> x4, Pallas kernels: 65.6 us -> 61.7 us  [product(): pl.pallas_call(product_body, out_shape=jax.ShapeDtypeStruct((2, height, w...]
    all_gather x5 -> x4, local copies, waits for them, and re-layouts: 15.5 us -> 16.2 us  [exchange(): line = lax.all_gather(piece, 'col', axis=0, axis_index_groups=groups)]
  transfers between devices with their start and end apart: 18 -> 16, of which waited for: 10 -> 9; matrix products, arithmetic and copies ran while one was open for 11% -> 11% of each run, Pallas kernels for 16% -> 13%
where the time goes in v4:
time: 393 us; the launch traced here: 392 us
  waiting for transfers between devices  248 us (63%)
  Pallas kernels  61.7 us (16%)
  local copies, waits for them, and re-layouts  24.9 us (6%)
  other arithmetic  22.6 us (6%)
  starting transfers between devices  21.5 us (5%)
  between operations  13.2 us (3%)
    all_gather x4, waiting for transfers between devices, exchange(): line = lax.all_gather(piece, 'col', axis=0, axis_index_groups=groups)  142 us
    pallas_call x4, Pallas kernels, product(): pl.pallas_call(product_body, out_shape=jax.ShapeDtypeStruct((2, height, w...  61.7 us
    all_to_all x4, waiting for transfers between devices, exchange(): block = lax.all_to_all(line, 'row', 0, 0)  59.7 us
    ppermute x4, waiting for transfers between devices, across(): return lax.ppermute(x, AXES, moves)  42.7 us
    all_to_all x4, starting transfers between devices, exchange(): block = lax.all_to_all(line, 'row', 0, 0)  16.9 us
    all_gather x4, local copies, waits for them, and re-layouts, exchange(): line = lax.all_gather(piece, 'col', axis=0, axis_index_groups=groups)  16.2 us
    convert_element_type x1, other arithmetic, split(): return (high.astype(jnp.bfloat16), (whole - high).astype(jnp.bfloat16))  8.37 us
  transfers between devices with their start and end apart: 16, of which 9 were waited for; matrix products, arithmetic and copies ran while one was open for 11% of the time, Pallas kernels for 13%

profile of v4, /device:TPU:0, one launch (start us, length us, event | category | flops | bytes accessed | tf_op | source)
XLA Modules:
  0.0 392.0 jit_solution(4313570220331528164)
XLA Ops:
  12.5 63.8 %all-gather.13.cloned.1.call-done = f32[1024,768]{0,1:T(8,128)} async-done(((f32[256,768]{0,1:T(8,128)}), f32[1024,768]{0,1:T(8,128)}) %all-gather.13.cloned.1.call-update) | async-done | bytes 3145744 | tf_op jit(solution)/shard_map/all_gather | solution.py:131
  76.3 3.5 copy.8
  79.9 3.7 all-to-all-start.2
  83.6 4.1 %broadcast_multiply_fusion = f32[768,1024]{1,0:T(8,128)} fusion(f32[768,1024]{1,0:T(8,128)} %param.2, f32[768]{0:T(1024)S(1)} %multiply_sqrt_fusion), kind=kLoop, calls=%fused_computation.4 | loop fusion | flops 786432 | bytes 6294528 | tf_op jit(solution)/shard_map/mul | solution.py:100
  91.2 74.9 %all-gather.9.cloned.1.call-done = f32[1536,768]{0,1:T(8,128)} async-done(((f32[384,768]{0,1:T(8,128)}), f32[1536,768]{0,1:T(8,128)}) %all-gather.9.cloned.1.call-update) | async-done | bytes 4718608 | tf_op jit(solution)/shard_map/all_gather | solution.py:131
  166.0 6.0 %copy.6 = f32[1536,768]{1,0:T(8,128)} copy(f32[1536,768]{0,1:T(8,128)} %all-gather.9.cloned.1.call-done) | data formatting | bytes 9437184 | tf_op jit(solution)/shard_map/all_gather | solution.py:131
  172.1 5.0 %all-to-all-start = ((f32[4,384,768]{2,1,0:T(8,128)}), f32[4,384,768]{2,1,0:T(8,128)}, u32[]{:S(2)}, u32[]{:S(2)}) async-start(f32[4,384,768]{2,1,0:T(8,128)} %bitcast.20), calls=%async_computation | async-start | bytes 9437184 | tf_op jit(solution)/shard_map/all_to_all | solution.py:135
  177.1 12.4 %collective-permute-done.2 = f32[768,1024]{1,0:T(8,128)} collective-permute-done((f32[768,1024]{1,0:T(8,128)}, f32[768,1024]{1,0:T(8,128)}, u32[]{:S(2)}, u32[]{:S(2)}) %collective-permute-start.2) | collective-permute-done | bytes 3145760 | tf_op jit(solution)/shard_map/ppermute | solution.py:93
  192.8 2.8 slice.25
  196.2 43.0 %all-to-all-done.mine_ref = f32[4,384,768]{2,1,0:T(8,128)} async-done(((f32[4,384,768]{2,1,0:T(8,128)}), f32[4,384,768]{2,1,0:T(8,128)}, u32[]{:S(2)}, u32[]{:S(2)}) %all-to-all-start) | async-done | bytes 4718624 | tf_op jit(solution)/shard_map/all_to_all | solution.py:135
  241.4 30.3 %collective-permute-done.1 = f32[768,512]{1,0:T(8,128)} collective-permute-done((f32[768,512]{1,0:T(8,128)}, f32[768,512]{1,0:T(8,128)}, u32[]{:S(2)}, u32[]{:S(2)}) %collective-permute-start.1) | collective-permute-done | bytes 1572896 | tf_op jit(solution)/shard_map/ppermute | solution.py:93
  274.8 8.4 %fusion = (bf16[4,768,1024]{2,1,0:T(8,128)(2,1)}, bf16[4,768,1024]{2,1,0:T(8,128)(2,1)}) fusion(f32[1,768,1024]{2,1,0:T(8,128)S(1)} %bitcast.23, f32[1,768,1024]{2,1,0:T(8,128)} %bitcast.12, f32[1,768,1024]{2,1,0:T(8,128)} %bitcast.11, f32[1,768,1024]{2,1,0:T(8,128)S(1)} %fusion.1), kind=kLoop, calls=%fused_computation.2 | loop fusion | flops 22020096 | bytes 25165824 | tf_op jit(solution)/shard_map/convert_element_type | solution.py:80
  283.2 15.2 %shard_map.28.refs_0_ = f32[2,1024,1024]{2,1,0:T(8,128)} custom-call(s32[2]{0:T(128)S(1)} %pad_add_fusion.where_ref, f32[4,256,768]{2,1,0:T(8,128)S(1)} %all-to-all-done.2.mine_ref, f32[4,256,768]{2,1,0:T(8,128)} %collective-permute-done.4.other_ref, bf16[4,768,1024]{2,1,0:T(8,128)(2,1)} %get-tuple-element.28.high_ref, ...), custom_call_target="tpu_custom_call" | custom-call | flops 805306368 | bytes 2097152 | tf_op jit(solution)/shard_map/pallas_call | solution.py:61
  298.4 3.6 copy.9
  302.0 3.7 all-to-all-start.3
  307.7 21.3 %shard_map.29.refs_0_ = f32[2,1024,1024]{2,1,0:T(8,128)} custom-call(s32[2]{0:T(128)S(1)} %pad_add_fusion.where_ref, f32[4,384,768]{2,1,0:T(8,128)} %all-to-all-done.mine_ref, f32[4,384,768]{2,1,0:T(8,128)} %collective-permute-done.5.other_ref, bf16[4,768,1024]{2,1,0:T(8,128)(2,1)} %get-tuple-element.28.high_ref, ...), custom_call_target="tpu_custom_call", output_to_operand_aliasing={{}: (5, {})} | custom-call | flops 1207959552 | bytes 3145728 | tf_op jit(solution)/shard_map/pallas_call | solution.py:61
  329.0 12.3 %all-to-all-done.3.mine_ref = f32[4,256,768]{2,1,0:T(8,128)S(1)} async-done(((f32[4,256,768]{2,1,0:T(8,128)}), f32[4,256,768]{2,1,0:T(8,128)S(1)}, u32[]{:S(2)}, u32[]{:S(2)}) %all-to-all-start.3) | async-done | bytes 3145760 | tf_op jit(solution)/shard_map/all_to_all | solution.py:135
  341.3 3.4 all-gather.11.cloned.1.call-done
  344.7 3.1 copy.7
  347.7 4.5 %all-to-all-start.1 = ((f32[4,128,768]{2,1,0:T(8,128)}), f32[4,128,768]{2,1,0:T(8,128)}, u32[]{:S(2)}, u32[]{:S(2)}) async-start(f32[4,128,768]{2,1,0:T(8,128)} %bitcast.24), calls=%async_computation.1 | async-start | bytes 3145728 | tf_op jit(solution)/shard_map/all_to_all | solution.py:135
  352.3 15.2 %shard_map.30.refs_0_ = f32[2,1024,1024]{2,1,0:T(8,128)} custom-call(s32[2]{0:T(128)S(1)} %pad_add_fusion.where_ref, f32[4,256,768]{2,1,0:T(8,128)S(1)} %all-to-all-done.3.mine_ref, f32[4,256,768]{2,1,0:T(8,128)} %collective-permute-done.6.other_ref, bf16[4,768,1024]{2,1,0:T(8,128)(2,1)} %get-tuple-element.28.high_ref, ...), custom_call_target="tpu_custom_call", output_to_operand_aliasing={{}: (5, {})} | custom-call | flops 805306368 | bytes 2097152 | tf_op jit(solution)/shard_map/pallas_call | solution.py:61
  367.5 4.4 %all-to-all-done.1.mine_ref = f32[4,128,768]{2,1,0:T(8,128)} async-done(((f32[4,128,768]{2,1,0:T(8,128)}), f32[4,128,768]{2,1,0:T(8,128)}, u32[]{:S(2)}, u32[]{:S(2)}) %all-to-all-start.1) | async-done | bytes 1572896 | tf_op jit(solution)/shard_map/all_to_all | solution.py:135
  371.9 3.6 collective-permute-done.7.other_ref
  375.5 10.0 %shard_map.31 = f32[2,1024,1024]{2,1,0:T(8,128)} custom-call(s32[2]{0:T(128)S(1)} %pad_add_fusion.where_ref, f32[4,128,768]{2,1,0:T(8,128)} %all-to-all-done.1.mine_ref, f32[4,128,768]{2,1,0:T(8,128)S(1)} %collective-permute-done.7.other_ref, bf16[4,768,1024]{2,1,0:T(8,128)(2,1)} %get-tuple-element.28.high_ref, ...), custom_call_target="tpu_custom_call", output_to_operand_aliasing={{}: (5, {})} | custom-call | flops 402653184 | bytes 1048576 | tf_op jit(solution)/shard_map/pallas_call | solution.py:61
  (32 shorter events, 20.6 us)
Async XLA Ops:
  6.5 69.8 %all-gather.13.cloned.1.call-start = ((), (), s32[]{:S(2)}) async-start(), calls=%async_computation.6 | async-start | bytes 3932160 | tf_op jit(solution)/shard_map/all_gather | solution.py:131
  10.0 156.0 %all-gather.9.cloned.1.call-start = ((), (), s32[]{:S(2)}) async-start(), calls=%async_computation.4 | async-start | bytes 5898240 | tf_op jit(solution)/shard_map/all_gather | solution.py:131
  79.9 92.2 %all-to-all-start.2 = ((f32[4,256,768]{2,1,0:T(8,128)}), f32[4,256,768]{2,1,0:T(8,128)S(1)}, u32[]{:S(2)}, u32[]{:S(2)}) async-start(f32[4,256,768]{2,1,0:T(8,128)} %bitcast.22), calls=%async_computation.2 | async-start | bytes 6291456 | tf_op jit(solution)/shard_map/all_to_all | solution.py:135
  87.7 101.8 %collective-permute-start.2 = (f32[768,1024]{1,0:T(8,128)}, f32[768,1024]{1,0:T(8,128)}, u32[]{:S(2)}, u32[]{:S(2)}) collective-permute-start(f32[768,1024]{1,0:T(8,128)} %broadcast_multiply_fusion), channel_id=1, source_target_pairs={{0,16},{1,17},{2,18},{3,19},{4,20},{5,21},{6,22},{7,23},{8,24},{9,... | collective-permute-start | bytes 9437192 | tf_op jit(solution)/shard_map/ppermute | solution.py:93
  89.7 99.8 %collective-permute-start = (f32[768,1024]{1,0:T(8,128)}, f32[768,1024]{1,0:T(8,128)}, u32[]{:S(2)}, u32[]{:S(2)}) collective-permute-start(f32[768,1024]{1,0:T(8,128)} %broadcast_multiply_fusion), channel_id=1, source_target_pairs={{0,8},{1,9},{2,10},{3,11},{4,12},{5,13},{6,14},{7,15},{8,0},{9,1},... | collective-permute-start | bytes 9437192 | tf_op jit(solution)/shard_map/ppermute | solution.py:93
  172.1 67.1 %all-to-all-start = ((f32[4,384,768]{2,1,0:T(8,128)}), f32[4,384,768]{2,1,0:T(8,128)}, u32[]{:S(2)}, u32[]{:S(2)}) async-start(f32[4,384,768]{2,1,0:T(8,128)} %bitcast.20), calls=%async_computation | async-start | bytes 9437184 | tf_op jit(solution)/shard_map/all_to_all | solution.py:135
  177.1 121.3 %all-gather.15.cloned.1.call-start = ((), (), s32[]{:S(2)}) async-start(), calls=%async_computation.7 | async-start | bytes 3932160 | tf_op jit(solution)/shard_map/all_gather | solution.py:131
  189.6 93.6 %collective-permute-start.4 = (f32[4,256,768]{2,1,0:T(8,128)S(1)}, f32[4,256,768]{2,1,0:T(8,128)}, u32[]{:S(2)}, u32[]{:S(2)}) collective-permute-start(f32[4,256,768]{2,1,0:T(8,128)S(1)} %all-to-all-done.2.mine_ref), channel_id=1, source_target_pairs={{0,1},{1,0},{2,3},{3,2},{4,5},{5,4},{6,7},{7,6},{8,9},{9,8},{10,11... | collective-permute-start | bytes 9437192 | tf_op jit(solution)/shard_map/ppermute | solution.py:97
  192.3 79.3 %collective-permute-start.1 = (f32[768,512]{1,0:T(8,128)}, f32[768,512]{1,0:T(8,128)}, u32[]{:S(2)}, u32[]{:S(2)}) collective-permute-start(f32[768,512]{1,0:T(8,128)} %slice.24), channel_id=1, source_target_pairs={{0,16},{1,17},{2,18},{3,19},{4,20},{5,21},{6,22},{7,23},{8,24},{9,... | collective-permute-start | bytes 4718600 | tf_op jit(solution)/shard_map/ppermute | solution.py:93
  195.7 77.6 %collective-permute-start.3 = (f32[768,512]{1,0:T(8,128)}, f32[768,512]{1,0:T(8,128)}, u32[]{:S(2)}, u32[]{:S(2)}) collective-permute-start(f32[768,512]{1,0:T(8,128)} %slice.25), channel_id=1, source_target_pairs={{0,8},{1,9},{2,10},{3,11},{4,12},{5,13},{6,14},{7,15},{8,0},{9,1},... | collective-permute-start | bytes 4718600 | tf_op jit(solution)/shard_map/ppermute | solution.py:93
  239.1 68.5 %collective-permute-start.5 = (f32[4,384,768]{2,1,0:T(8,128)}, f32[4,384,768]{2,1,0:T(8,128)}, u32[]{:S(2)}, u32[]{:S(2)}) collective-permute-start(f32[4,384,768]{2,1,0:T(8,128)} %all-to-all-done.mine_ref), channel_id=1, source_target_pairs={{0,1},{1,0},{2,3},{3,2},{4,5},{5,4},{6,7},{7,6},{8,9},{9,8},{10,11... | collective-permute-start | bytes 14155784 | tf_op jit(solution)/shard_map/ppermute | solution.py:97
  302.0 39.3 %all-to-all-start.3 = ((f32[4,256,768]{2,1,0:T(8,128)}), f32[4,256,768]{2,1,0:T(8,128)S(1)}, u32[]{:S(2)}, u32[]{:S(2)}) async-start(f32[4,256,768]{2,1,0:T(8,128)} %bitcast.21), calls=%async_computation.3 | async-start | bytes 6291456 | tf_op jit(solution)/shard_map/all_to_all | solution.py:135
  305.7 39.0 %all-gather.11.cloned.1.call-start = ((), (), s32[]{:S(2)}) async-start(), calls=%async_computation.5 | async-start | bytes 1966080 | tf_op jit(solution)/shard_map/all_gather | solution.py:131
  341.3 11.0 %collective-permute-start.6 = (f32[4,256,768]{2,1,0:T(8,128)S(1)}, f32[4,256,768]{2,1,0:T(8,128)}, u32[]{:S(2)}, u32[]{:S(2)}) collective-permute-start(f32[4,256,768]{2,1,0:T(8,128)S(1)} %all-to-all-done.3.mine_ref), channel_id=1, source_target_pairs={{0,1},{1,0},{2,3},{3,2},{4,5},{5,4},{6,7},{7,6},{8,9},{9,8},{10,11... | collective-permute-start | bytes 9437192 | tf_op jit(solution)/shard_map/ppermute | solution.py:97
  347.7 24.1 %all-to-all-start.1 = ((f32[4,128,768]{2,1,0:T(8,128)}), f32[4,128,768]{2,1,0:T(8,128)}, u32[]{:S(2)}, u32[]{:S(2)}) async-start(f32[4,128,768]{2,1,0:T(8,128)} %bitcast.24), calls=%async_computation.1 | async-start | bytes 3145728 | tf_op jit(solution)/shard_map/all_to_all | solution.py:135
  371.9 3.6 collective-permute-start.7
Sparse Core Ops, SparseCore 0:
  10.1 66.1 all-gather.12
  77.9 88.0 all-gather.8
  189.7 60.3 all-gather.14
  307.8 36.8 all-gather.10
